TPU v7x, 32 devices: a whole 2x2x4 slice. The times are simulated.
32 devices in a mesh: grp: 2 (over x), seq: 16 (over z, y, core).
Axes of the slice: x: 2, y: 2, z: 4, core: 2. Of those that a mesh axis runs over, the one named last changes fastest.
Arguments:
- queries: bfloat16 [2, 2048, 4608], P('grp', 'seq'), may hold values from -16 to 16
- latents: bfloat16 [2, 2048, 576], P('grp', 'seq'), may hold values from -6 to 6
- cotangent: bfloat16 [2, 2048, 4096], P('grp', 'seq'), may hold values from -6 to 6
- comp_weight: float32 [32, 576], replicated, may hold values from -1 to 1
- sel_idx: int32 [2, 32, 64], P('grp', 'seq'), may hold values from 0 to 63, as said below
- sel_count: int32 [2, 32], P('grp', 'seq'), may hold values from 0 to 62, as said below
Outputs:
- attended: bfloat16 [2, 2048, 4096], P('grp', 'seq')
- query_grads: bfloat16 [2, 2048, 4608], P('grp', 'seq')
- latent_grads: float32 [2, 2048, 576], P('grp', 'seq')
- comp_weight_grads: float32 [32, 576], replicated
Inputs may be any that keep to these rules, and one draw needn't show every extreme that they name: `sel_idx`: in query block r the first sel_count entries are distinct compressed-latent numbers below r * 2; the other entries are 0 and unused. sel_count of query block r is at most min(64, r * 2); the last query block of every sequence reaches min(64, 62).
All inputs are finite; a program needn't handle non-finite values.
Results may differ from a plain program's by a relative error of at most 0.019.
Values may be sent and summed in bfloat16 or wider, within the bound.
A program may use at most 64 MiB of HBM per device.

v0:
```python
import jax
import jax.numpy as jnp
from jax import lax
from jax.sharding import PartitionSpec as P

DL = 512
DR = 64
H = 8
QB = 64
CS = 32
SEL = 64
WIN = 512
DK = 576


score_scale = 192.0 ** (-0.5)


def shifted(block, axis, distance):
    devices = range(lax.axis_size(axis))
    route = [(i - distance, i) for i in devices if i - distance in devices]
    return lax.ppermute(block, axis, route)


def forward_block(query_rows, grad_rows, key_rows, allowed):
    scores = (
        jnp.einsum("qhd,kd->qhk", query_rows, key_rows, preferred_element_type=jnp.float32)
        * score_scale
    )
    scores = jnp.where(allowed[:, None, :], scores, -jnp.inf)
    row_max = jnp.max(scores, axis=2, keepdims=True)
    expo_part = jnp.exp(scores - row_max)
    row_sum = jnp.sum(expo_part, axis=2, keepdims=True)
    weights = expo_part / row_sum
    rounded = weights.astype(jnp.bfloat16)
    value_rows = key_rows[:, :DL]
    context = jnp.einsum("qhk,kd->qhd", rounded, value_rows, preferred_element_type=jnp.float32)
    prob_grad = jnp.einsum("qhd,kd->qhk", grad_rows, value_rows, preferred_element_type=jnp.float32)
    row_dot = jnp.sum(grad_rows.astype(jnp.float32) * context, axis=2, keepdims=True)
    dscore = (weights * (prob_grad - row_dot)).astype(jnp.bfloat16)
    query_grad = (
        jnp.einsum("qhk,kd->qhd", dscore, key_rows, preferred_element_type=jnp.float32)
        * score_scale
    )
    return (context, query_grad, dscore, rounded, row_max, row_sum, row_dot)


def key_terms(query_rows, grad_rows, dscore, rounded):
    key_grad = (
        jnp.einsum("qhk,qhd->kd", dscore, query_rows, preferred_element_type=jnp.float32)
        * score_scale
    )
    value_grad = jnp.einsum("qhk,qhd->kd", rounded, grad_rows, preferred_element_type=jnp.float32)
    return key_grad + jnp.pad(value_grad, ((0, 0), (0, DR)))


def recompute_terms(query_rows, grad_rows, piece_rows, piece_ok, row_max, row_sum, row_dot):
    scores = (
        jnp.einsum("qhd,kd->qhk", query_rows, piece_rows, preferred_element_type=jnp.float32)
        * score_scale
    )
    scores = jnp.where(piece_ok[None, None, :], scores, -jnp.inf)
    weights = jnp.exp(scores - row_max) / row_sum
    rounded = weights.astype(jnp.bfloat16)
    prob_grad = jnp.einsum(
        "qhd,kd->qhk", grad_rows, piece_rows[:, :DL], preferred_element_type=jnp.float32
    )
    dscore = (weights * (prob_grad - row_dot)).astype(jnp.bfloat16)
    return key_terms(query_rows, grad_rows, dscore, rounded)


def body(queries, latents, cotangent, comp_weight, sel_idx, sel_count):
    tok_rows = latents.shape[1]
    base_pos = lax.axis_index("seq") * tok_rows
    local_blocks = tok_rows // QB
    comp_local = tok_rows // CS
    total_comp = comp_local * lax.axis_size("seq")
    hop_count = (WIN + tok_rows - 1) // tok_rows
    lead_rows = hop_count * tok_rows
    own_latent = latents[0]
    query_all = queries[0].reshape(tok_rows, H, DK)
    grad_all = cotangent[0].reshape(tok_rows, H, DL)
    block_view = own_latent.astype(jnp.float32).reshape(comp_local, CS, DK)
    compressed_local = jnp.sum(block_view * comp_weight[None], axis=1).astype(jnp.bfloat16)
    compressed = lax.all_gather(compressed_local, "seq", axis=0, tiled=True)
    earlier = []
    for distance in range(hop_count, 0, -1):
        earlier.append(shifted(own_latent, "seq", distance))
    extended = jnp.concatenate(earlier + [own_latent], axis=0)
    ext_grad = jnp.zeros((lead_rows + tok_rows, DK), jnp.float32)
    comp_ids = jnp.arange(total_comp, dtype=jnp.int32)
    slot_ids = jnp.arange(SEL, dtype=jnp.int32)
    within = jnp.arange(QB, dtype=jnp.int32)
    offsets = jnp.arange(WIN + QB, dtype=jnp.int32)
    contexts = []
    query_grads = []
    records = []
    for block_id in range(local_blocks):
        first_row = block_id * QB
        query_rows = query_all[first_row : first_row + QB]
        grad_rows = grad_all[first_row : first_row + QB]
        window_start = first_row + lead_rows - WIN
        window_rows = extended[window_start : window_start + WIN + QB]
        query_pos = base_pos + first_row + within
        key_pos = base_pos + first_row - WIN + offsets
        window_ok = (
            (key_pos[None, :] <= query_pos[:, None])
            & (key_pos[None, :] > query_pos[:, None] - WIN)
            & (key_pos[None, :] >= 0)
        )
        chosen = sel_idx[0, block_id]
        live_slots = slot_ids < sel_count[0, block_id]
        one_hot = (chosen[:, None] == comp_ids[None, :]) & live_slots[:, None]
        selected = jnp.any(one_hot, axis=0)
        key_rows = jnp.concatenate([compressed, window_rows], axis=0)
        allowed = jnp.concatenate(
            [jnp.broadcast_to(selected[None, :], (QB, total_comp)), window_ok], axis=1
        )
        context, query_grad, dscore, rounded, row_max, row_sum, row_dot = forward_block(
            query_rows, grad_rows, key_rows, allowed
        )
        window_grad = key_terms(
            query_rows, grad_rows, dscore[:, :, total_comp:], rounded[:, :, total_comp:]
        )
        records.append((query_rows, grad_rows, selected, row_max, row_sum, row_dot))
        ext_grad = ext_grad.at[window_start : window_start + WIN + QB].add(window_grad)
        contexts.append(context.astype(jnp.bfloat16).reshape(QB, H * DL))
        query_grads.append(query_grad.astype(jnp.bfloat16).reshape(QB, H * DK))
    partial_sum = jnp.zeros((lax.axis_size("seq") * comp_local, DK), jnp.float32)
    for saved_block in records:
        query_rows, grad_rows, selected, row_max, row_sum, row_dot = saved_block
        partial_sum = partial_sum + recompute_terms(
            query_rows, grad_rows, compressed, selected, row_max, row_sum, row_dot
        )
    comp_grad = lax.psum_scatter(partial_sum, "seq", scatter_dimension=0, tiled=True)
    latent_grad = ext_grad[lead_rows:]
    for distance in range(hop_count, 0, -1):
        segment_start = (hop_count - distance) * tok_rows
        segment = ext_grad[segment_start : segment_start + tok_rows]
        latent_grad = latent_grad + shifted(segment.astype(jnp.bfloat16), "seq", -distance).astype(
            segment.dtype
        )
    latent_grad = latent_grad + (comp_weight[None] * comp_grad[:, None, :]).reshape(tok_rows, DK)
    weight_part = jnp.sum(comp_grad[:, None, :] * block_view, axis=0)
    weight_grad = lax.psum(weight_part, ("grp", "seq"))
    attended = jnp.concatenate(contexts, axis=0)[None]
    query_out = jnp.concatenate(query_grads, axis=0)[None]
    return (attended, query_out, latent_grad[None], weight_grad)


def solution(mesh):
    in_specs = (
        P("grp", "seq", None),
        P("grp", "seq", None),
        P("grp", "seq", None),
        P(),
        P("grp", "seq", None),
        P("grp", "seq"),
    )
    out_specs = (P("grp", "seq", None), P("grp", "seq", None), P("grp", "seq", None), P())
    return jax.shard_map(body, mesh=mesh, in_specs=in_specs, out_specs=out_specs, check_vma=False)
```

profile of v0, /device:TPU:0, one launch (start us, length us, event | category | flops | bytes accessed | tf_op | source)
XLA Modules:
  0.0 317.5 jit_solution(11290838901009748866)
XLA Ops:
  7.2 3.0 collective-permute-start.3
  10.2 4.4 %collective-permute-start.2 = (bf16[128,576]{0,1:T(8,128)(2,1)}, bf16[128,576]{0,1:T(8,128)(2,1)}, u32[]{:S(2)}, u32[]{:S(2)}) collective-permute-start(bf16[128,576]{0,1:T(8,128)(2,1)} %bitcast.149), channel_id=1, source_target_pairs={{0,2},{1,3},{2,4},{3,5},{4,6},{5,7},{6,8},{7,9},{8,10},{9,11},{10,... | collective-permute-start | bytes 442376 | tf_op jit(solution)/shard_map/ppermute | solution.py:22
  14.7 4.4 %collective-permute-start.1 = (bf16[128,576]{0,1:T(8,128)(2,1)}, bf16[128,576]{0,1:T(8,128)(2,1)}, u32[]{:S(2)}, u32[]{:S(2)}) collective-permute-start(bf16[128,576]{0,1:T(8,128)(2,1)} %bitcast.150), channel_id=1, source_target_pairs={{0,3},{1,4},{2,5},{3,6},{4,7},{5,8},{6,9},{7,10},{8,11},{9,12},{10... | collective-permute-start | bytes 442376 | tf_op jit(solution)/shard_map/ppermute | solution.py:22
  19.1 3.5 %collective-permute-start = (bf16[128,576]{0,1:T(8,128)(2,1)}, bf16[128,576]{0,1:T(8,128)(2,1)}, u32[]{:S(2)}, u32[]{:S(2)}) collective-permute-start(bf16[128,576]{0,1:T(8,128)(2,1)} %bitcast.151), channel_id=1, source_target_pairs={{0,4},{1,5},{2,6},{3,7},{4,8},{5,9},{6,10},{7,11},{8,12},{9,13},{1... | collective-permute-start | bytes 442376 | tf_op jit(solution)/shard_map/ppermute | solution.py:22
  22.6 1.1 copy.92
  23.7 0.8 slice_bitcast_fusion.6
  24.5 1.3 fusion.103
  25.8 0.6 iota_compare_fusion.3
  26.5 0.7 iota_compare_fusion.2
  27.3 0.6 copy-done.29
  27.9 1.3 fusion.100
  29.4 0.7 pad_add_fusion
  30.2 0.7 pad_add_fusion.1
  31.0 18.8 %all-gather = bf16[16,4,576]{2,1,0:T(4,128)(2,1)S(1)} all-gather(bf16[1,4,576]{2,1,0:T(4,128)(2,1)S(1)} %bitcast.154), channel_id=1, replica_groups=mesh['grp'=2,'seq'=16] {'seq'}, dimensions={0}, use_global_device_ids=true | all-gather | bytes 78336 | tf_op jit(solution)/shard_map/all_gather | solution.py:85
  49.9 0.7 reshape.162
  50.5 0.8 copy.93
  51.7 0.5 slice.126
  52.2 0.5 slice.132
  52.8 0.7 dynamic-slice.15
  54.1 0.9 constant_dynamic-update-slice_fusion.4
  55.1 0.9 constant_dynamic-update-slice_fusion.3
  56.0 0.9 constant_dynamic-update-slice_fusion.2
  57.0 0.9 constant_dynamic-update-slice_fusion.1
  58.0 0.4 fusion.102
  58.5 0.4 copy-done.20
  58.9 1.0 fusion.104
  60.9 2.1 multiply_reduce_fusion
  63.1 1.8 convolution_bitcast_fusion
  64.9 0.5 fusion.24
  65.7 1.0 fusion.105
  67.3 0.5 fusion.20
  68.2 1.5 multiply_reduce_fusion.1
  69.7 0.7 convolution_bitcast_fusion.1
  70.5 1.0 convolution_bitcast_fusion.4
  71.4 1.4 copy.107
  72.9 3.1 fusion.12
  76.0 2.5 fusion.35
  78.5 3.1 fusion.14
  81.7 2.3 reshape.148
  83.9 1.2 copy.139
  85.5 2.4 fusion.11
  87.9 0.9 copy-done.15
  88.8 1.9 fusion.13
  90.6 2.3 reshape.147
  92.9 2.0 copy.138
  94.9 2.2 fusion.33
  97.2 2.1 fusion.2
  99.3 1.0 fusion.106
  100.3 0.9 scatter-add.6
  101.3 0.9 fusion.101
  102.2 7.8 %scatter-add.9 = bf16[640,576]{0,1:T(8,128)(2,1)} dynamic-update-slice(bf16[640,576]{0,1:T(8,128)(2,1)} %scatter-add.6, f32[576,576]{0,1:T(8,128)S(1)} %get-tuple-element.54, s32[]{:T(128)} %constant.86.clone.1, s32[]{:T(128)} %constant.81.clone.1) | dynamic-update-slice | bytes 2654212 | tf_op jit(solution)/shard_map/scatter-add | solution.py:126
  110.0 1.6 slice.208
  111.7 1.3 collective-permute-start.4
  112.9 1.3 collective-permute-start.5
  114.2 1.3 collective-permute-start.7
  115.5 1.3 collective-permute-start.6
  116.9 1.1 maximum_bitcast_fusion
  118.0 1.0 maximum_bitcast_fusion.1
  119.0 63.5 %all-reduce.11.cloned.1.call-done = f32[64,576]{1,0:T(8,128)} async-done(((f32[64,576]{1,0:T(8,128)}), f32[64,576]{1,0:T(8,128)}) %all-reduce.11.cloned.1.call-update) | async-done | bytes 147472
  182.6 0.7 constant_dynamic-slice_fusion
  183.3 0.7 fusion.75
  184.2 1.9 fusion.80
  186.1 123.1 %all-reduce.9.cloned.1.call-done = f32[32,576]{1,0:T(8,128)} async-done(((f32[32,576]{1,0:T(8,128)}), f32[32,576]{1,0:T(8,128)}) %all-reduce.9.cloned.1.call-update) | async-done | bytes 73744 | tf_op jit(solution)/shard_map/psum | solution.py:145
  309.1 1.5 copy.201
  (101 shorter events, 3.9 us)
Async XLA Ops:
  7.2 175.4 %all-reduce.11.cloned.1.call-start = ((), (), s32[]{:S(2)}) async-start(), calls=%async_computation.1 | async-start | bytes 327680
  7.2 49.8 %collective-permute-start.3 = (bf16[128,576]{0,1:T(8,128)(2,1)}, bf16[128,576]{0,1:T(8,128)(2,1)}, u32[]{:S(2)}, u32[]{:S(2)}) collective-permute-start(bf16[128,576]{0,1:T(8,128)(2,1)} %bitcast.148), channel_id=1, source_target_pairs={{0,1},{1,2},{2,3},{3,4},{4,5},{5,6},{6,7},{7,8},{8,9},{9,10},{10,1... | collective-permute-start | bytes 442376 | tf_op jit(solution)/shard_map/ppermute | solution.py:22
  10.2 45.8 %collective-permute-start.2 = (bf16[128,576]{0,1:T(8,128)(2,1)}, bf16[128,576]{0,1:T(8,128)(2,1)}, u32[]{:S(2)}, u32[]{:S(2)}) collective-permute-start(bf16[128,576]{0,1:T(8,128)(2,1)} %bitcast.149), channel_id=1, source_target_pairs={{0,2},{1,3},{2,4},{3,5},{4,6},{5,7},{6,8},{7,9},{8,10},{9,11},{10,... | collective-permute-start | bytes 442376 | tf_op jit(solution)/shard_map/ppermute | solution.py:22
  14.7 40.4 %collective-permute-start.1 = (bf16[128,576]{0,1:T(8,128)(2,1)}, bf16[128,576]{0,1:T(8,128)(2,1)}, u32[]{:S(2)}, u32[]{:S(2)}) collective-permute-start(bf16[128,576]{0,1:T(8,128)(2,1)} %bitcast.150), channel_id=1, source_target_pairs={{0,3},{1,4},{2,5},{3,6},{4,7},{5,8},{6,9},{7,10},{8,11},{9,12},{10... | collective-permute-start | bytes 442376 | tf_op jit(solution)/shard_map/ppermute | solution.py:22
  19.1 35.0 %collective-permute-start = (bf16[128,576]{0,1:T(8,128)(2,1)}, bf16[128,576]{0,1:T(8,128)(2,1)}, u32[]{:S(2)}, u32[]{:S(2)}) collective-permute-start(bf16[128,576]{0,1:T(8,128)(2,1)} %bitcast.151), channel_id=1, source_target_pairs={{0,4},{1,5},{2,6},{3,7},{4,8},{5,9},{6,10},{7,11},{8,12},{9,13},{1... | collective-permute-start | bytes 442376 | tf_op jit(solution)/shard_map/ppermute | solution.py:22
  23.7 7.2 %copy-start.8 = (bf16[1,128,576]{2,1,0:T(8,128)(2,1)}, bf16[1,128,576]{2,1,0:T(8,128)(2,1)S(1)}, u32[]{:S(2)}) copy-start(bf16[1,128,576]{2,1,0:T(8,128)(2,1)S(1)} %copy.92) | copy-start | bytes 442372
  23.7 5.4 %copy-start.10 = (bf16[1,128,4608]{2,1,0:T(8,128)(2,1)S(1)}, bf16[1,128,4608]{2,1,0:T(8,128)(2,1)}, u32[]{:S(2)}) copy-start(bf16[1,128,4608]{2,1,0:T(8,128)(2,1)} %param.10) | copy-start | bytes 3538948
  27.3 0.6 copy-start.29
  27.3 0.6 copy-start.31
  29.1 1.8 copy-start.17
  51.7 1.1 copy-start.33
  52.2 5.7 %copy-start.16 = (bf16[1,128,576]{1,2,0:T(8,128)(2,1)S(1)}, bf16[1,128,576]{1,2,0:T(8,128)(2,1)}, u32[]{:S(2)}) copy-start(bf16[1,128,576]{1,2,0:T(8,128)(2,1)} %param.11) | copy-start | bytes 442372
  52.7 12.2 %copy-start.3 = (bf16[64,8,576]{2,1,0:T(8,128)(2,1)}, bf16[64,8,576]{2,1,0:T(8,128)(2,1)S(1)}, u32[]{:S(2)}) copy-start(bf16[64,8,576]{2,1,0:T(8,128)(2,1)S(1)} %slice.132) | copy-start | bytes 1769476
  58.0 0.9 copy-start.20
  58.0 0.9 copy-start.24
  58.4 2.5 copy-start.13
  58.4 9.7 %copy-start.11 = (bf16[576,576]{0,1:T(8,128)(2,1)}, bf16[576,576]{0,1:T(8,128)(2,1)S(1)}, u32[]{:S(2)}) copy-start(bf16[576,576]{0,1:T(8,128)(2,1)S(1)} %get-tuple-element.39) | copy-start | bytes 1990660
  59.9 1.1 copy-start.1
  59.9 5.0 %copy-start.25 = (f32[64,8]{0,1:T(8,128)}, f32[64,8]{0,1:T(8,128)S(1)}, u32[]{:S(2)}) copy-start(f32[64,8]{0,1:T(8,128)S(1)} %get-tuple-element.47) | copy-start | bytes 6148
  60.3 4.6 %copy-start.27 = (f32[64,8]{0,1:T(8,128)}, f32[64,8]{0,1:T(8,128)S(1)}, u32[]{:S(2)}) copy-start(f32[64,8]{0,1:T(8,128)S(1)} %fusion.28) | copy-start | bytes 6148
  63.1 1.8 copy-start.22
  63.1 1.8 copy-start.32
  64.9 0.8 copy-start.23
  65.4 5.0 %copy-start.19 = (f32[64,64,8]{1,0,2:T(8,128)}, f32[64,64,8]{1,0,2:T(8,128)S(1)}, u32[]{:S(2)}) copy-start(f32[64,64,8]{1,0,2:T(8,128)S(1)} %fusion.24) | copy-start | bytes 393220
  66.7 1.2 copy-start
  66.7 0.7 copy-start.30
  69.7 3.1 copy-start.26
  69.7 3.1 copy-start.28
  85.5 3.3 %copy-start.12 = (bf16[576,576]{0,1:T(8,128)(2,1)S(1)}, bf16[576,576]{0,1:T(8,128)(2,1)}, u32[]{:S(2)}) copy-start(bf16[576,576]{0,1:T(8,128)(2,1)} %copy-done.11) | copy-start | bytes 1990660
  85.5 3.3 %copy-start.21 = (bf16[64,576]{0,1:T(8,128)(2,1)S(1)}, bf16[64,576]{0,1:T(8,128)(2,1)}, u32[]{:S(2)}) copy-start(bf16[64,576]{0,1:T(8,128)(2,1)} %copy.93) | copy-start | bytes 221188
  87.9 0.9 copy-start.15
  97.1 212.0 %all-reduce.9.cloned.1.call-start = ((), (), s32[]{:S(2)}) async-start(), calls=%async_computation | async-start | bytes 163840 | tf_op jit(solution)/shard_map/psum | solution.py:145
  97.2 2.1 copy-start.2
  97.2 2.1 copy-start.4
  97.2 2.1 copy-start.14
  102.2 14.6 %copy-start.5 = (bf16[64,4608]{1,0:T(8,128)(2,1)S(1)}, bf16[64,4608]{1,0:T(8,128)(2,1)}, u32[]{:S(2)}) copy-start(bf16[64,4608]{1,0:T(8,128)(2,1)} %reshape.148) | copy-start | bytes 1769476
  102.2 14.6 %copy-start.6 = (bf16[64,4608]{1,0:T(8,128)(2,1)S(1)}, bf16[64,4608]{1,0:T(8,128)(2,1)}, u32[]{:S(2)}) copy-start(bf16[64,4608]{1,0:T(8,128)(2,1)} %reshape.147) | copy-start | bytes 1769476
  110.0 8.0 %copy-start.7 = (bf16[8,8,8,512]{3,1,2,0:T(8,128)(2,1)S(1)}, bf16[8,8,8,512]{3,1,2,0:T(8,128)(2,1)}, u32[]{:S(2)}) copy-start(bf16[8,8,8,512]{3,1,2,0:T(8,128)(2,1)} %copy.138) | copy-start | bytes 1572868
  111.7 72.5 %collective-permute-start.4 = (bf16[128,576]{0,1:T(8,128)(2,1)}, bf16[128,576]{0,1:T(8,128)(2,1)S(1)}, u32[]{:S(2)}, u32[]{:S(2)}) collective-permute-start(bf16[128,576]{0,1:T(8,128)(2,1)} %slice.208), channel_id=1, source_target_pairs={{4,0},{5,1},{6,2},{7,3},{8,4},{9,5},{10,6},{11,7},{12,8},{13,9},{1... | collective-permute-start | bytes 442376 | tf_op jit(solution)/shard_map/ppermute | solution.py:22
  112.9 71.2 %collective-permute-start.5 = (bf16[128,576]{0,1:T(8,128)(2,1)}, bf16[128,576]{0,1:T(8,128)(2,1)S(1)}, u32[]{:S(2)}, u32[]{:S(2)}) collective-permute-start(bf16[128,576]{0,1:T(8,128)(2,1)} %get-tuple-element.36), channel_id=1, source_target_pairs={{3,0},{4,1},{5,2},{6,3},{7,4},{8,5},{9,6},{10,7},{11,8},{12,9},{13... | collective-permute-start | bytes 442376 | tf_op jit(solution)/shard_map/ppermute | solution.py:22
  114.2 69.9 %collective-permute-start.7 = (bf16[128,576]{0,1:T(8,128)(2,1)}, bf16[128,576]{0,1:T(8,128)(2,1)}, u32[]{:S(2)}, u32[]{:S(2)}) collective-permute-start(bf16[128,576]{0,1:T(8,128)(2,1)} %get-tuple-element.37), channel_id=1, source_target_pairs={{1,0},{2,1},{3,2},{4,3},{5,4},{6,5},{7,6},{8,7},{9,8},{10,9},{11,1... | collective-permute-start | bytes 442376 | tf_op jit(solution)/shard_map/ppermute | solution.py:22
  115.5 68.6 %collective-permute-start.6 = (bf16[128,576]{0,1:T(8,128)(2,1)}, bf16[128,576]{0,1:T(8,128)(2,1)}, u32[]{:S(2)}, u32[]{:S(2)}) collective-permute-start(bf16[128,576]{0,1:T(8,128)(2,1)} %get-tuple-element.38), channel_id=1, source_target_pairs={{2,0},{3,1},{4,2},{5,3},{6,4},{7,5},{8,6},{9,7},{10,8},{11,9},{12,... | collective-permute-start | bytes 442376 | tf_op jit(solution)/shard_map/ppermute | solution.py:22
  118.0 65.3 %copy-start.9 = (bf16[1,128,576]{2,1,0:T(8,128)(2,1)S(1)}, bf16[1,128,576]{2,1,0:T(8,128)(2,1)}, u32[]{:S(2)}) copy-start(bf16[1,128,576]{2,1,0:T(8,128)(2,1)} %copy-done.8) | copy-start | bytes 442372
  118.0 65.3 %copy-start.18 = (f32[32,576]{1,0:T(8,128)S(1)}, f32[32,576]{1,0:T(8,128)}, u32[]{:S(2)}) copy-start(f32[32,576]{1,0:T(8,128)} %param.13) | copy-start | bytes 221188
Sparse Core Ops, SparseCore 0:
  97.3 85.2 all-reduce.10
  188.7 120.3 all-reduce.8
where the time goes:
time: 320 us; the launch traced here: 317 us
  waiting for transfers between devices  187 us (58%)
  local copies, waits for them, and re-layouts  38 us (12%)
  matrix products  28.7 us (9%)
  starting transfers between devices  20.6 us (6%)
  blocking collectives  18.8 us (6%)
  between operations  15.3 us (5%)
  other arithmetic  9.29 us (3%)
    psum x1, waiting for transfers between devices, body(): weight_grad = lax.psum(weight_part, ('grp', 'seq'))  123 us
    unnamed x3, waiting for transfers between devices  63.6 us
    ppermute x8, starting transfers between devices, shifted(): return lax.ppermute(block, axis, route)  20.5 us
    all_gather x1, blocking collectives, body(): compressed = lax.all_gather(compressed_local, 'seq', axis=0, tiled=True)  18.8 us
    unnamed x83, local copies, waits for them, and re-layouts  15.7 us
    scatter-add x2, local copies, waits for them, and re-layouts, body(): ext_grad.at[window_start:window_start + WIN + QB].add(window_grad)  8.72 us
    dot_general x4, matrix products, key_terms(): jnp.einsum('qhk,qhd->kd', dscore, query_rows, preferred_element_type=jnp....  7.8 us
  transfers between devices with their start and end apart: 10, of which 2 were waited for; matrix products, arithmetic and copies ran while one was open for 11% of the time, Pallas kernels for 0%

commit v1 on v0

v1 whole, which is shorter than its diff:
```python
import functools

import jax
import jax.numpy as jnp
from jax import lax
from jax.experimental import pallas as pl
from jax.experimental.pallas import tpu as pltpu
from jax.sharding import PartitionSpec as P

DL = 512
DR = 64
H = 8
QB = 64
CS = 32
WIN = 512
DK = 576
LANES = 128
WIDE = 640
PIECES = WIDE // LANES
SLOT = 8
MASKED = -1e30

MESH = pl.DeviceIdType.MESH
BF16 = jnp.bfloat16
F32 = jnp.float32
score_scale = 192.0 ** (-0.5)


def round_up(value, step):
    return (value + step - 1) // step * step


def dot_nn(a, b):
    return lax.dot_general(a, b, (((1,), (0,)), ((), ())), preferred_element_type=F32)


def dot_nt(a, b):
    return lax.dot_general(a, b, (((1,), (1,)), ((), ())), preferred_element_type=F32)


def dot_tn(a, b):
    return lax.dot_general(a, b, (((0,), (0,)), ((), ())), preferred_element_type=F32)


def piece_width(j):
    return min(LANES, DK - j * LANES)


def gather_kernel(n, hop, tok, cl, lat_ref, cw_ref, win_ref, comp_ref, tmp, wsend, wrecv, csend, crecv):
    seq = lax.axis_index("seq")
    grp = lax.axis_index("grp")
    barrier = pltpu.get_barrier_semaphore()

    def greet(k, c):
        pl.semaphore_signal(
            barrier, inc=1, device_id=(grp, lax.rem(seq + k, n)), device_id_type=MESH
        )
        return c

    lax.fori_loop(1, n, greet, 0)

    tmp[...] = jnp.zeros_like(tmp)
    for b in range(cl):
        block = lat_ref[pl.ds(b * CS, CS), :].astype(F32) * cw_ref[...]
        row = jnp.sum(block, axis=0, keepdims=True)
        for j in range(PIECES):
            w = piece_width(j)
            tmp[pl.ds(j * cl + b, 1), pl.ds(0, w)] = row[:, j * LANES : j * LANES + w]
    comp_ref[seq] = tmp[...].astype(BF16)
    pl.semaphore_wait(barrier, n - 1)

    def comp_copy(peer):
        return pltpu.make_async_remote_copy(
            src_ref=comp_ref.at[seq],
            dst_ref=comp_ref.at[seq],
            send_sem=csend.at[peer],
            recv_sem=crecv.at[seq],
            device_id=(grp, peer),
            device_id_type=MESH,
        )

    def comp_arrival(peer):
        return pltpu.make_async_remote_copy(
            src_ref=comp_ref.at[peer],
            dst_ref=comp_ref.at[peer],
            send_sem=csend.at[peer],
            recv_sem=crecv.at[peer],
            device_id=(grp, peer),
            device_id_type=MESH,
        )

    def win_copy(d):
        return pltpu.make_async_remote_copy(
            src_ref=lat_ref,
            dst_ref=win_ref.at[pl.ds((hop - d) * tok, tok)],
            send_sem=wsend.at[d],
            recv_sem=wrecv.at[d],
            device_id=(grp, lax.rem(seq + d, n)),
            device_id_type=MESH,
        )

    for d in range(1, hop + 1):
        pl.when(seq + d < n)(lambda d=d: win_copy(d).start())

    def send_comp(k, c):
        comp_copy(lax.rem(seq + k, n)).start()
        return c

    lax.fori_loop(1, n, send_comp, 0)
    for d in range(1, hop + 1):

        @pl.when(seq < d)
        def _(d=d):
            win_ref[pl.ds((hop - d) * tok, tok), :] = jnp.zeros((tok, DK), BF16)

    def wait_comp(k, c):
        comp_arrival(lax.rem(seq + k, n)).wait_recv()
        comp_copy(lax.rem(seq + k, n)).wait_send()
        return c

    lax.fori_loop(1, n, wait_comp, 0)
    for d in range(1, hop + 1):
        pl.when(seq >= d)(lambda d=d: win_copy(d).wait_recv())
        pl.when(seq + d < n)(lambda d=d: win_copy(d).wait_send())


def attend_kernel(
    n, hop, tok, cl,
    q_ref, cot_ref, lat_ref, win_ref, comp_ref, idx_ref, cnt_ref,
    att_ref, qg_ref, wing_ref, own_ref, cg_ref,
    kk, kf, qq, cc, bias, ds_ref, pp, dq, pack,
):
    cp = bias.shape[1] - round_up(hop * tok + tok, LANES)
    nk = bias.shape[1]
    lead = hop * tok
    ext = lead + tok
    half = (H // 2) * tok
    pair = 2 * DK
    seq = lax.axis_index("seq")
    pr = pack.shape[1]

    kf[pl.ds(0, cp), :] = jnp.zeros((cp, WIDE), F32)

    def unpack(o, c):
        packed = comp_ref[o].astype(F32)
        for j in range(PIECES):
            kf[pl.ds(pl.multiple_of(o * SLOT, SLOT), cl), pl.ds(j * LANES, LANES)] = packed[
                j * cl : (j + 1) * cl, :
            ]
        return c

    lax.fori_loop(0, n, unpack, 0)
    kf[pl.ds(cp, ext), pl.ds(DL, LANES)] = jnp.zeros((ext, LANES), F32)
    kf[pl.ds(cp, lead), pl.ds(0, DK)] = win_ref[...].astype(F32)
    kf[pl.ds(cp + lead, tok), pl.ds(0, DK)] = lat_ref[...].astype(F32)
    if nk > cp + ext:
        kf[pl.ds(cp + ext, nk - cp - ext), :] = jnp.zeros((nk - cp - ext, WIDE), F32)
    kk[0] = kf[...].astype(BF16)
    kk[1] = pltpu.roll(kf[...], DR, 1).astype(BF16)

    for m in range(H // 2):
        for p in range(2):
            rows = pl.ds(p * half + m * tok, tok)
            qq[rows, :] = q_ref[:, pl.ds(m * pair + p * DL, WIDE)]
            cc[rows, :] = cot_ref[:, pl.ds((2 * m + p) * DL, DL)]

    blocks = tok // QB
    slots = idx_ref.shape[1]
    key_id = lax.broadcasted_iota(jnp.int32, (cp, slots), 0)
    in_slot = key_id % SLOT
    comp_id = jnp.where(in_slot < cl, (key_id // SLOT) * cl + in_slot, -1)
    slot_id = lax.broadcasted_iota(jnp.int32, (cp, slots), 1)
    for r in range(blocks):
        chosen = idx_ref[pl.ds(r, 1), :]
        hit = (comp_id == chosen) & (slot_id < cnt_ref[0, r])
        hit = jnp.where(hit, 1.0, 0.0).astype(BF16)
        count = dot_nt(jnp.ones((QB, slots), BF16), hit)
        bias[pl.ds(r * QB, QB), pl.ds(0, cp)] = jnp.where(count > 0.5, 0.0, MASKED)
    wide = nk - cp
    row = lax.broadcasted_iota(jnp.int32, (tok, wide), 0)
    col = lax.broadcasted_iota(jnp.int32, (tok, wide), 1)
    shift = lead - WIN
    ok = (col > row + shift) & (col <= row + lead) & (col - lead + seq * tok >= 0)
    bias[:, pl.ds(cp, wide)] = jnp.where(ok, 0.0, MASKED)

    step = min(256, half)
    heads = step // tok
    for c in range(2 * half // step):
        p = c * step // half
        rows = pl.ds(c * step, step)
        keys = kk[p]
        values = kk[0, :, pl.ds(0, DL)]
        s = dot_nt(qq[rows, :], keys) * score_scale
        s = (s.reshape(heads, tok, nk) + bias[...][None]).reshape(step, nk)
        e = jnp.exp(s - jnp.max(s, axis=1, keepdims=True))
        w = e * (1.0 / jnp.sum(e, axis=1, keepdims=True))
        rounded = w.astype(BF16)
        pp[rows, :] = rounded
        context = dot_nn(rounded, values)
        grads = cc[rows, :]
        row_dot = jnp.sum(grads.astype(F32) * context, axis=1, keepdims=True)
        dscore = (w * (dot_nt(grads, values) - row_dot)).astype(BF16)
        ds_ref[rows, :] = dscore
        dq[rows, :] = dot_nn(dscore, keys) * score_scale
        for i in range(heads):
            m = (c * step - p * half) // tok + i
            att_ref[:, pl.ds((2 * m + p) * DL, DL)] = context[i * tok : (i + 1) * tok].astype(BF16)

    for m in range(H // 2):
        even = pl.ds(m * tok, tok)
        odd = pl.ds(half + m * tok, tok)
        qg_ref[:, pl.ds(m * pair, DL)] = dq[even, pl.ds(0, DL)].astype(BF16)
        qg_ref[:, pl.ds(m * pair + DL, LANES)] = (
            dq[even, pl.ds(DL, LANES)] + dq[odd, pl.ds(0, LANES)]
        ).astype(BF16)
        qg_ref[:, pl.ds(m * pair + WIDE, DL)] = dq[odd, pl.ds(LANES, DL)].astype(BF16)

    for start in range(0, nk, 256):
        size = min(256, nk - start)
        cols = pl.ds(start, size)
        even = dot_tn(ds_ref[pl.ds(0, half), cols], qq[pl.ds(0, half), :])
        odd = dot_tn(ds_ref[pl.ds(half, half), cols], qq[pl.ds(half, half), :])
        value = dot_tn(pp[:, cols], cc[...])
        total = (even + pltpu.roll(odd, WIDE - DR, 1)) * score_scale
        kf[cols, pl.ds(0, DL)] = total[:, :DL] + value
        kf[cols, pl.ds(DL, LANES)] = total[:, DL:]

    wing_ref[...] = kf[pl.ds(cp, lead), pl.ds(0, DK)].astype(BF16)
    own_ref[...] = kf[pl.ds(cp + lead, tok), pl.ds(0, DK)]
    pack[...] = jnp.zeros_like(pack)

    def pack_one(o, c):
        for j in range(PIECES):
            pack[o, pl.ds(j * cl, cl), :] = kf[
                pl.ds(pl.multiple_of(o * SLOT, SLOT), cl), pl.ds(j * LANES, LANES)
            ]
        return c

    lax.fori_loop(0, n, pack_one, 0)
    cg_ref[...] = pack[...].astype(BF16)


def scatter_kernel(
    n, groups, hop, tok, cl, owners,
    cg_ref, wing_ref, own_ref, lat_ref, cw_ref,
    lg_ref, wg_ref,
    crecv_buf, wrecv_buf, tot, cgrad, part, precv, pout,
    csend, crecv, wsend, wrecv, psend, precv_sem, osend, orecv,
):
    seq = lax.axis_index("seq")
    grp = lax.axis_index("grp")
    count = n * groups
    me = grp * n + seq
    per = CS // owners * SLOT
    barrier = pltpu.get_barrier_semaphore()

    def where(peer):
        return (peer // n, peer % n)

    def greet(k, c):
        pl.semaphore_signal(
            barrier, inc=1, device_id=where((me + k) % count), device_id_type=MESH
        )
        return c

    lax.fori_loop(1, count, greet, 0)
    pl.semaphore_wait(barrier, count - 1)

    def comp_copy(peer):
        return pltpu.make_async_remote_copy(
            src_ref=cg_ref.at[peer],
            dst_ref=crecv_buf.at[seq],
            send_sem=csend.at[peer],
            recv_sem=crecv.at[seq],
            device_id=(grp, peer),
            device_id_type=MESH,
        )

    def comp_arrival(peer):
        return pltpu.make_async_remote_copy(
            src_ref=cg_ref.at[peer],
            dst_ref=crecv_buf.at[peer],
            send_sem=csend.at[peer],
            recv_sem=crecv.at[peer],
            device_id=(grp, peer),
            device_id_type=MESH,
        )

    def win_copy(d):
        rows = pl.ds((hop - d) * tok, tok)
        return pltpu.make_async_remote_copy(
            src_ref=wing_ref.at[rows],
            dst_ref=wrecv_buf.at[rows],
            send_sem=wsend.at[d],
            recv_sem=wrecv.at[d],
            device_id=(grp, (seq + n - d) % n),
            device_id_type=MESH,
        )

    def part_copy(peer):
        return pltpu.make_async_remote_copy(
            src_ref=part.at[pl.ds(peer * per, per)],
            dst_ref=precv.at[me],
            send_sem=psend.at[peer],
            recv_sem=precv_sem.at[me],
            device_id=where(peer),
            device_id_type=MESH,
        )

    def part_arrival(peer):
        return pltpu.make_async_remote_copy(
            src_ref=part.at[pl.ds(0, per)],
            dst_ref=precv.at[peer],
            send_sem=psend.at[0],
            recv_sem=precv_sem.at[peer],
            device_id=where(peer),
            device_id_type=MESH,
        )

    def out_copy(peer):
        return pltpu.make_async_remote_copy(
            src_ref=pout.at[pl.ds(me * per, per)],
            dst_ref=pout.at[pl.ds(me * per, per)],
            send_sem=osend.at[peer],
            recv_sem=orecv.at[me],
            device_id=where(peer),
            device_id_type=MESH,
        )

    def out_arrival(peer):
        rows = pl.ds(peer * per, per)
        return pltpu.make_async_remote_copy(
            src_ref=pout.at[rows],
            dst_ref=pout.at[rows],
            send_sem=osend.at[peer],
            recv_sem=orecv.at[peer],
            device_id=where(peer),
            device_id_type=MESH,
        )

    def each(size, base, work):
        def one(k, c):
            work((base + k) % size)
            return c

        lax.fori_loop(1, size, one, 0)

    def to_owners(work):
        def one(peer):
            if owners == count:
                work(peer)
            else:
                pl.when(peer < owners)(lambda: work(peer))

        each(count, me, one)

    def if_owner(work):
        if owners == count:
            work()
        else:
            pl.when(me < owners)(work)

    each(n, seq, lambda peer: comp_copy(peer).start())
    for d in range(1, hop + 1):
        pl.when(seq >= d)(lambda d=d: win_copy(d).start())
    crecv_buf[seq] = cg_ref[seq]
    part[...] = jnp.zeros_like(part)
    each(n, seq, lambda peer: comp_arrival(peer).wait_recv())

    tot[...] = jnp.sum(crecv_buf[...].astype(F32), axis=0)
    for j in range(PIECES):
        cgrad[pl.ds(0, cl), pl.ds(j * LANES, LANES)] = tot[pl.ds(j * cl, cl), :]
    weight = jnp.zeros((CS, DK), F32)
    for b in range(cl):
        weight = weight + cgrad[pl.ds(b, 1), pl.ds(0, DK)] * lat_ref[pl.ds(b * CS, CS), :].astype(F32)
    for j in range(PIECES):
        w = piece_width(j)
        part[pl.ds(j, CS, stride=SLOT), pl.ds(0, w)] = weight[:, j * LANES : j * LANES + w]
    to_owners(lambda peer: part_copy(peer).start())

    for d in range(1, hop + 1):

        @pl.when(seq + d >= n)
        def _(d=d):
            wrecv_buf[pl.ds((hop - d) * tok, tok), :] = jnp.zeros((tok, DK), BF16)

    for b in range(cl):
        rows = pl.ds(b * CS, CS)
        lg_ref[rows, :] = own_ref[rows, :] + cw_ref[...] * cgrad[pl.ds(b, 1), pl.ds(0, DK)]

    @if_owner
    def _():
        precv[me] = part[pl.ds(pl.multiple_of(me * per, per), per), :]
        each(count, me, lambda peer: part_arrival(peer).wait_recv())
        pout[pl.ds(pl.multiple_of(me * per, per), per), :] = jnp.sum(precv[...], axis=0)
        each(count, me, lambda peer: out_copy(peer).start())

    for d in range(1, hop + 1):
        pl.when(seq + d < n)(lambda d=d: win_copy(d).wait_recv())
    far = lg_ref[...]
    for d in range(1, hop + 1):
        far = far + wrecv_buf[pl.ds((hop - d) * tok, tok), :].astype(F32)
    lg_ref[...] = far

    to_owners(lambda peer: out_arrival(peer).wait_recv())
    for j in range(PIECES):
        w = piece_width(j)
        wg_ref[:, pl.ds(j * LANES, w)] = pout[pl.ds(j, CS, stride=SLOT), :][:, :w]

    each(n, seq, lambda peer: comp_copy(peer).wait_send())
    for d in range(1, hop + 1):
        pl.when(seq >= d)(lambda d=d: win_copy(d).wait_send())
    to_owners(lambda peer: part_copy(peer).wait_send())
    if_owner(lambda: each(count, me, lambda peer: out_copy(peer).wait_send()))


def vmem(count):
    return [pl.BlockSpec(memory_space=pltpu.VMEM)] * count


def body(n, groups, queries, latents, cotangent, comp_weight, sel_idx, sel_count):
    tok = latents.shape[1]
    hop = (WIN + tok - 1) // tok
    lead = hop * tok
    cl = tok // CS
    pr = round_up(cl * PIECES, 16)
    cp = round_up(n * SLOT, LANES)
    nk = cp + round_up(lead + tok, LANES)
    count = n * groups
    owners = min(CS, count)
    per = CS // owners * SLOT
    own = latents[0]
    dma = pltpu.SemaphoreType.DMA

    win, comp = pl.pallas_call(
        functools.partial(gather_kernel, n, hop, tok, cl),
        out_shape=(
            jax.ShapeDtypeStruct((lead, DK), BF16),
            jax.ShapeDtypeStruct((n, pr, LANES), BF16),
        ),
        in_specs=vmem(2),
        out_specs=tuple(vmem(2)),
        scratch_shapes=[
            pltpu.VMEM((pr, LANES), F32),
            dma((hop + 1,)),
            dma((hop + 1,)),
            dma((n,)),
            dma((n,)),
        ],
        compiler_params=pltpu.CompilerParams(collective_id=0, has_side_effects=True),
    )(own, comp_weight)

    att, qg, wing, own_grad, cg = pl.pallas_call(
        functools.partial(attend_kernel, n, hop, tok, cl),
        out_shape=(
            jax.ShapeDtypeStruct((tok, H * DL), BF16),
            jax.ShapeDtypeStruct((tok, H * DK), BF16),
            jax.ShapeDtypeStruct((lead, DK), BF16),
            jax.ShapeDtypeStruct((tok, DK), F32),
            jax.ShapeDtypeStruct((n, pr, LANES), BF16),
        ),
        in_specs=vmem(6) + [pl.BlockSpec(memory_space=pltpu.SMEM)],
        out_specs=tuple(vmem(5)),
        scratch_shapes=[
            pltpu.VMEM((2, nk, WIDE), BF16),
            pltpu.VMEM((nk, WIDE), F32),
            pltpu.VMEM((H * tok, WIDE), BF16),
            pltpu.VMEM((H * tok, DL), BF16),
            pltpu.VMEM((tok, nk), F32),
            pltpu.VMEM((H * tok, nk), BF16),
            pltpu.VMEM((H * tok, nk), BF16),
            pltpu.VMEM((H * tok, WIDE), F32),
            pltpu.VMEM((n, pr, LANES), F32),
        ],
        compiler_params=pltpu.CompilerParams(vmem_limit_bytes=56 * 2**20),
    )(queries[0], cotangent[0], own, win, comp, sel_idx[0], sel_count)

    lat_grad, weight_grad = pl.pallas_call(
        functools.partial(scatter_kernel, n, groups, hop, tok, cl, owners),
        out_shape=(
            jax.ShapeDtypeStruct((tok, DK), F32),
            jax.ShapeDtypeStruct((CS, DK), F32),
        ),
        in_specs=vmem(5),
        out_specs=tuple(vmem(2)),
        scratch_shapes=[
            pltpu.VMEM((n, pr, LANES), BF16),
            pltpu.VMEM((lead, DK), BF16),
            pltpu.VMEM((pr, LANES), F32),
            pltpu.VMEM((SLOT, WIDE), F32),
            pltpu.VMEM((CS * SLOT, LANES), F32),
            pltpu.VMEM((count, per, LANES), F32),
            pltpu.VMEM((CS * SLOT, LANES), F32),
            dma((n,)),
            dma((n,)),
            dma((hop + 1,)),
            dma((hop + 1,)),
            dma((count,)),
            dma((count,)),
            dma((count,)),
            dma((count,)),
        ],
        compiler_params=pltpu.CompilerParams(collective_id=1, has_side_effects=True),
    )(cg, wing, own_grad, own, comp_weight)
    return (att[None], qg[None], lat_grad[None], weight_grad)


def solution(mesh):
    in_specs = (
        P("grp", "seq", None),
        P("grp", "seq", None),
        P("grp", "seq", None),
        P(),
        P("grp", "seq", None),
        P("grp", "seq"),
    )
    out_specs = (P("grp", "seq", None), P("grp", "seq", None), P("grp", "seq", None), P())
    return jax.shard_map(
        functools.partial(body, mesh.shape["seq"], mesh.shape["grp"]),
        mesh=mesh,
        in_specs=in_specs,
        out_specs=out_specs,
        check_vma=False,
    )
```

time: 320 us -> 76.8 us (0.24)
  waiting for transfers between devices: 187 us -> 0 us
  Pallas kernels: 0 us -> 70.8 us
  local copies, waits for them, and re-layouts: 38 us -> 5.08 us
  matrix products: 28.7 us -> 0 us
  starting transfers between devices: 20.6 us -> 0 us
  blocking collectives: 18.8 us -> 0 us
  between operations: 15.3 us -> 0.65 us
  other arithmetic: 9.29 us -> 0 us
    psum x1 -> x0, waiting for transfers between devices: 123 us -> none  [body(): weight_grad = lax.psum(weight_part, ('grp', 'seq'))]
    pallas_call x0 -> x3, Pallas kernels: none -> 70.8 us  [the longest x1 41.3 us: body(): pl.pallas_call(functools.partial(scatter_kernel, n, groups, hop, tok, cl,...]
    unnamed x3 -> x0, waiting for transfers between devices: 63.6 us -> none
    dot_general x18 -> x0, matrix products: 28.7 us -> none  [the longest x4 7.8 us: key_terms(): jnp.einsum('qhk,qhd->kd', dscore, query_rows, preferred_element_type=jnp....]
    ppermute x8 -> x0, starting transfers between devices: 20.5 us -> none  [shifted(): return lax.ppermute(block, axis, route)]
    all_gather x1 -> x0, blocking collectives: 18.8 us -> none  [body(): compressed = lax.all_gather(compressed_local, 'seq', axis=0, tiled=True)]
    unnamed x83 -> x3, local copies, waits for them, and re-layouts: 15.7 us -> 5.08 us
    scatter-add x2 -> x0, local copies, waits for them, and re-layouts: 8.72 us -> none  [body(): ext_grad.at[window_start:window_start + WIN + QB].add(window_grad)]
  transfers between devices with their start and end apart: 10 -> 0, of which waited for: 2 -> 0; matrix products, arithmetic and copies ran while one was open for 11% -> 0% of each run, Pallas kernels for 0% -> 0%
where the time goes in v1:
time: 76.8 us; the launch traced here: 76.5 us
  Pallas kernels  70.8 us (92%)
  local copies, waits for them, and re-layouts  5.08 us (7%)
    pallas_call x1, Pallas kernels, body(): pl.pallas_call(functools.partial(scatter_kernel, n, groups, hop, tok, cl,...  41.3 us
    pallas_call x1, Pallas kernels, body(): pl.pallas_call(functools.partial(gather_kernel, n, hop, tok, cl), out_sha...  17.3 us
    pallas_call x1, Pallas kernels, body(): pl.pallas_call(functools.partial(attend_kernel, n, hop, tok, cl), out_sha...  12.2 us
    unnamed x3, local copies, waits for them, and re-layouts  5.08 us

profile of v1, /device:TPU:0, one launch (start us, length us, event | category | flops | bytes accessed | tf_op | source)
XLA Modules:
  0.0 76.5 jit_solution(12902843171020461969)
XLA Ops:
  0.6 1.7 %copy.10 = bf16[1,128,576]{2,1,0:T(8,128)(2,1)} copy(bf16[1,128,576]{1,2,0:T(8,128)(2,1)} %param.7) | data formatting | bytes 294912 | tf_op args[1]
  2.3 17.3 %shard_map.93 = (bf16[512,576]{1,0:T(8,128)(2,1)}, bf16[16,32,128]{2,1,0:T(8,128)(2,1)}) custom-call(bf16[128,576]{1,0:T(8,128)(2,1)} %bitcast.7, f32[32,576]{1,0:T(8,128)} %cw_ref.3), custom_call_target="tpu_custom_call" | custom-call | tf_op jit(solution)/shard_map/pallas_call | solution.py:435
  19.7 12.2 %shard_map.94 = (bf16[128,4096]{1,0:T(8,128)(2,1)}, bf16[128,4608]{1,0:T(8,128)(2,1)}, bf16[512,576]{1,0:T(8,128)(2,1)}, f32[128,576]{1,0:T(8,128)}, bf16[16,32,128]{2,1,0:T(8,128)(2,1)}) custom-call(bf16[128,4608]{1,0:T(8,128)(2,1)} %bitcast.10, bf16[128,4096]{1,0:T(8,128)(2,1)} %bitcast.11, bf16[128,576]{1,0:T(8,128)(2,1)} %bitcast.8, ...), custom_call_target="tpu_custom_call" | custom-call | tf_op jit(solution)/shard_map/pallas_call | solution.py:453
  31.8 41.3 %shard_map.95 = (f32[128,576]{1,0:T(8,128)}, f32[32,576]{1,0:T(8,128)}) custom-call(bf16[16,32,128]{2,1,0:T(8,128)(2,1)} %get-tuple-element.17.cg_ref, bf16[512,576]{1,0:T(8,128)(2,1)} %get-tuple-element.18.wing_ref, f32[128,576]{1,0:T(8,128)} %get-tuple-element.19.own_ref, bf16[128,576]{1,0:T(8,128)(2,1)} %bitcast.9, f32[32,576]{1,0:T(8,128)} %cw_ref.3), custom_call_target="tpu_custom_call" | custom-call | tf_op jit(solution)/shard_map/pallas_call | solution.py:478
  73.2 1.8 %copy.11 = f32[1,128,576]{1,2,0:T(8,128)} copy(f32[1,128,576]{2,1,0:T(8,128)} %bitcast.12) | data formatting | bytes 589824
  75.0 1.5 %copy.13 = f32[32,576]{1,0:T(8,128)} copy(f32[32,576]{1,0:T(8,128)} %get-tuple-element.33) | data formatting | bytes 147456

commit v2 on v1

v2 whole, which is shorter than its diff:
```python
import functools

import jax
import jax.numpy as jnp
from jax import lax
from jax.experimental import pallas as pl
from jax.experimental.pallas import tpu as pltpu
from jax.sharding import PartitionSpec as P

DL = 512
DR = 64
H = 8
QB = 64
CS = 32
WIN = 512
DK = 576
LANES = 128
WIDE = 640
PIECES = WIDE // LANES
SLOT = 8
MASKED = -1e30

MESH = pl.DeviceIdType.MESH
BF16 = jnp.bfloat16
F32 = jnp.float32
score_scale = 192.0 ** (-0.5)


def round_up(value, step):
    return (value + step - 1) // step * step


def dot_nn(a, b):
    return lax.dot_general(a, b, (((1,), (0,)), ((), ())), preferred_element_type=F32)


def dot_nt(a, b):
    return lax.dot_general(a, b, (((1,), (1,)), ((), ())), preferred_element_type=F32)


def dot_tn(a, b):
    return lax.dot_general(a, b, (((0,), (0,)), ((), ())), preferred_element_type=F32)


def piece_width(j):
    return min(LANES, DK - j * LANES)


def each(size, base, work):
    def one(k, c):
        work((base + k) % size)
        return c

    lax.fori_loop(1, size, one, 0)


def kernel(
    n, groups, hop, tok, cl, owners,
    q_ref, cot_ref, lat_ref, cw_ref, idx_ref, cnt_ref,
    att_ref, qg_ref, lg_ref, wg_ref,
    qq, cc, win, comp, tmp, kk, kf, bias, ds_ref, pp, dq, att_buf, qg_buf,
    pack, cg, crecv_buf, cgrad, part, precv, pout, wing, srecv, wrecv,
    load_sem, save_sem,
    gc_send, gc_recv, gw_send, gw_recv, gs_send, gs_recv,
    rc_send, rc_recv, rs_send, rs_recv, rw_send, rw_recv,
    p_send, p_recv, o_send, o_recv,
):
    seq = lax.axis_index("seq")
    grp = lax.axis_index("grp")
    count = n * groups
    me = grp * n + seq
    parity = seq % 2
    base = seq - parity
    sibling = base + 1 - parity
    per = CS // owners * SLOT
    nk = bias.shape[1]
    lead = hop * tok
    ext = lead + tok
    cp = nk - round_up(ext, LANES)
    half = (H // 2) * tok
    pair = 2 * DK
    reach = hop // 2

    def where(peer):
        return (peer // n, peer % n)

    def remote(src, dst, send, recv, device):
        return pltpu.make_async_remote_copy(
            src_ref=src, dst_ref=dst, send_sem=send, recv_sem=recv,
            device_id=device, device_id_type=MESH,
        )

    def segment(d):
        return pl.ds((hop - d) * tok, tok)

    barrier = pltpu.get_barrier_semaphore()
    each(
        count, me,
        lambda peer: pl.semaphore_signal(
            barrier, inc=1, device_id=where(peer), device_id_type=MESH
        ),
    )

    loads = []
    for m in range(H // 2):
        for p in range(2):
            rows = pl.ds(p * half + m * tok, tok)
            at = 2 * (2 * m + p)
            loads.append(
                pltpu.make_async_copy(
                    q_ref.at[:, pl.ds(m * pair + p * DL, WIDE)], qq.at[rows], load_sem.at[at]
                )
            )
            loads.append(
                pltpu.make_async_copy(
                    cot_ref.at[:, pl.ds((2 * m + p) * DL, DL)], cc.at[rows], load_sem.at[at + 1]
                )
            )
    for load in loads:
        load.start()

    tmp[...] = jnp.zeros_like(tmp)
    for b in range(cl):
        block = lat_ref[pl.ds(b * CS, CS), :].astype(F32) * cw_ref[...]
        row = jnp.sum(block, axis=0, keepdims=True)
        for j in range(PIECES):
            w = piece_width(j)
            tmp[pl.ds(j * cl + b, 1), pl.ds(0, w)] = row[:, j * LANES : j * LANES + w]
    comp[seq] = tmp[...].astype(BF16)
    pl.semaphore_wait(barrier, count - 1)

    def comp_send(peer):
        return remote(comp.at[seq], comp.at[seq], gc_send.at[peer], gc_recv.at[seq], (grp, peer))

    def comp_wait(peer):
        return remote(comp.at[peer], comp.at[peer], gc_send.at[peer], gc_recv.at[peer], (grp, peer))

    def win_copy(k):
        return remote(
            lat_ref, win.at[segment(2 * k)], gw_send.at[k], gw_recv.at[k],
            (grp, (seq + 2 * k) % n),
        )

    def pass_on(k, d):
        src = lat_ref if k == 0 else win.at[segment(2 * k)]
        return remote(src, win.at[segment(d)], gs_send.at[k], gs_recv.at[d], (grp, sibling))

    def forwarded(work):
        for k in range(reach + 1):
            if k < reach:
                pl.when((parity == 0) & (base >= 2 * k))(lambda k=k: work(k, 2 * k + 1, True))
            if k > 0:
                pl.when((parity == 1) & (base >= 2 * k))(lambda k=k: work(k, 2 * k - 1, False))

    for k in range(reach, 0, -1):
        pl.when(base + 2 * k < n)(lambda k=k: win_copy(k).start())
    pl.when(parity == 0)(lambda: pass_on(0, 1).start())
    each(n, seq, lambda peer: comp_send(peer).start())

    for d in range(1, hop + 1):

        @pl.when(seq < d)
        def _(d=d):
            win[segment(d), :] = jnp.zeros((tok, DK), BF16)

    blocks = tok // QB
    slots = idx_ref.shape[1]
    key_id = lax.broadcasted_iota(jnp.int32, (cp, slots), 0)
    in_slot = key_id % SLOT
    comp_id = jnp.where(in_slot < cl, (key_id // SLOT) * cl + in_slot, -1)
    slot_id = lax.broadcasted_iota(jnp.int32, (cp, slots), 1)
    for r in range(blocks):
        chosen = idx_ref[pl.ds(r, 1), :]
        hit = (comp_id == chosen) & (slot_id < cnt_ref[0, r])
        hit = jnp.where(hit, 1.0, 0.0).astype(BF16)
        live = dot_nt(jnp.ones((QB, slots), BF16), hit)
        bias[pl.ds(r * QB, QB), pl.ds(0, cp)] = jnp.where(live > 0.5, 0.0, MASKED)
    wide = nk - cp
    row = lax.broadcasted_iota(jnp.int32, (tok, wide), 0)
    col = lax.broadcasted_iota(jnp.int32, (tok, wide), 1)
    shift = lead - WIN
    ok = (col > row + shift) & (col <= row + lead) & (col - lead + seq * tok >= 0)
    bias[:, pl.ds(cp, wide)] = jnp.where(ok, 0.0, MASKED)
    kf[pl.ds(0, cp), :] = jnp.zeros((cp, WIDE), F32)
    kf[pl.ds(cp, ext), pl.ds(DL, LANES)] = jnp.zeros((ext, LANES), F32)
    kf[pl.ds(cp + lead, tok), pl.ds(0, DK)] = lat_ref[...].astype(F32)
    if nk > cp + ext:
        kf[pl.ds(cp + ext, nk - cp - ext), :] = jnp.zeros((nk - cp - ext, WIDE), F32)
    pack[...] = jnp.zeros_like(pack)
    part[...] = jnp.zeros_like(part)

    for k in range(1, reach + 1):

        @pl.when(base >= 2 * k)
        def _(k=k):
            win_copy(k).wait_recv()
            if k < reach:
                pl.when(parity == 0)(lambda: pass_on(k, 2 * k + 1).start())
            pl.when(parity == 1)(lambda: pass_on(k, 2 * k - 1).start())

    each(n, seq, lambda peer: comp_wait(peer).wait_recv())

    def unpack(o, c):
        packed = comp[o].astype(F32)
        for j in range(PIECES):
            kf[pl.ds(pl.multiple_of(o * SLOT, SLOT), cl), pl.ds(j * LANES, LANES)] = packed[
                j * cl : (j + 1) * cl, :
            ]
        return c

    lax.fori_loop(0, n, unpack, 0)

    def sibling_arrival(k, d):
        pass_on(k, d).wait_recv()

    for k in range(reach + 1):
        if k < reach:
            pl.when((parity == 1) & (base >= 2 * k))(lambda k=k: sibling_arrival(k, 2 * k + 1))
        if k > 0:
            pl.when((parity == 0) & (base >= 2 * k))(lambda k=k: sibling_arrival(k, 2 * k - 1))
    kf[pl.ds(cp, lead), pl.ds(0, DK)] = win[...].astype(F32)
    kk[0] = kf[...].astype(BF16)
    kk[1] = pltpu.roll(kf[...], DR, 1).astype(BF16)
    for load in loads:
        load.wait()

    step = min(256, half)
    heads = step // tok
    for c in range(2 * half // step):
        p = c * step // half
        rows = pl.ds(c * step, step)
        keys = kk[p]
        values = kk[0, :, pl.ds(0, DL)]
        s = dot_nt(qq[rows, :], keys) * score_scale
        s = (s.reshape(heads, tok, nk) + bias[...][None]).reshape(step, nk)
        e = jnp.exp(s - jnp.max(s, axis=1, keepdims=True))
        w = e * (1.0 / jnp.sum(e, axis=1, keepdims=True))
        rounded = w.astype(BF16)
        pp[rows, :] = rounded
        context = dot_nn(rounded, values)
        grads = cc[rows, :]
        row_dot = jnp.sum(grads.astype(F32) * context, axis=1, keepdims=True)
        dscore = (w * (dot_nt(grads, values) - row_dot)).astype(BF16)
        ds_ref[rows, :] = dscore
        dq[rows, :] = dot_nn(dscore, keys) * score_scale
        for i in range(heads):
            m = (c * step - p * half) // tok + i
            att_buf[:, pl.ds((2 * m + p) * DL, DL)] = context[i * tok : (i + 1) * tok].astype(BF16)

    save_att = pltpu.make_async_copy(att_buf, att_ref, save_sem.at[0])
    save_att.start()

    def key_pass(start):
        size = min(256, nk - start)
        cols = pl.ds(start, size)
        even = dot_tn(ds_ref[pl.ds(0, half), cols], qq[pl.ds(0, half), :])
        odd = dot_tn(ds_ref[pl.ds(half, half), cols], qq[pl.ds(half, half), :])
        value = dot_tn(pp[:, cols], cc[...])
        total = (even + pltpu.roll(odd, WIDE - DR, 1)) * score_scale
        kf[cols, pl.ds(0, DL)] = total[:, :DL] + value
        kf[cols, pl.ds(DL, LANES)] = total[:, DL:]

    def seg_grad(d):
        return kf[pl.ds(cp + (hop - d) * tok, tok), pl.ds(0, DK)]

    def sum_send(peer):
        return remote(cg.at[peer], crecv_buf.at[seq], rc_send.at[peer], rc_recv.at[seq], (grp, peer))

    def sum_wait(peer):
        return remote(
            cg.at[peer], crecv_buf.at[peer], rc_send.at[peer], rc_recv.at[peer], (grp, peer)
        )

    def to_sibling(k, d):
        return remote(
            wing.at[segment(d)], srecv.at[k], rs_send.at[k], rs_recv.at[k], (grp, sibling)
        )

    def to_source(k):
        return remote(
            wing.at[segment(2 * k)], wrecv.at[k - 1], rw_send.at[k], rw_recv.at[k],
            (grp, (seq + n - 2 * k) % n),
        )

    def part_copy(peer):
        return remote(
            part.at[pl.ds(peer * per, per)], precv.at[me], p_send.at[peer], p_recv.at[me],
            where(peer),
        )

    def part_wait(peer):
        return remote(
            part.at[pl.ds(0, per)], precv.at[peer], p_send.at[0], p_recv.at[peer], where(peer)
        )

    def out_copy(peer):
        rows = pl.ds(me * per, per)
        return remote(pout.at[rows], pout.at[rows], o_send.at[peer], o_recv.at[me], where(peer))

    def out_wait(peer):
        rows = pl.ds(peer * per, per)
        return remote(pout.at[rows], pout.at[rows], o_send.at[peer], o_recv.at[peer], where(peer))

    def to_owners(work):
        def one(peer):
            if owners == count:
                work(peer)
            else:
                pl.when(peer < owners)(lambda: work(peer))

        each(count, me, one)

    def if_owner(work):
        if owners == count:
            work()
        else:
            pl.when(me < owners)(work)

    done = 0
    while done < cp:
        key_pass(done)
        done += 256

    def pack_one(o, c):
        for j in range(PIECES):
            pack[o, pl.ds(j * cl, cl), :] = kf[
                pl.ds(pl.multiple_of(o * SLOT, SLOT), cl), pl.ds(j * LANES, LANES)
            ]
        return c

    lax.fori_loop(0, n, pack_one, 0)
    cg[...] = pack[...].astype(BF16)
    crecv_buf[seq] = cg[seq]
    each(n, seq, lambda peer: sum_send(peer).start())

    while done < nk:
        key_pass(done)
        done += 256

    def send_sibling(k, d, unused):
        wing[segment(d), :] = seg_grad(d).astype(BF16)
        to_sibling(k, d).start()

    def back(work):
        for k in range(reach, -1, -1):
            if k > 0:
                pl.when((parity == 0) & (base >= 2 * k))(lambda k=k: work(k, 2 * k - 1, True))
            if k < reach:
                pl.when((parity == 1) & (base >= 2 * k))(lambda k=k: work(k, 2 * k + 1, False))

    back(send_sibling)

    @pl.when((parity == 0) & (base >= hop))
    def _():
        wing[segment(hop), :] = seg_grad(hop).astype(BF16)
        to_source(reach).start()

    each(n, seq, lambda peer: sum_wait(peer).wait_recv())
    total = jnp.sum(crecv_buf[...].astype(F32), axis=0)
    for j in range(PIECES):
        cgrad[pl.ds(0, cl), pl.ds(j * LANES, LANES)] = total[j * cl : (j + 1) * cl, :]
    weight = jnp.zeros((CS, DK), F32)
    for b in range(cl):
        weight = weight + cgrad[pl.ds(b, 1), pl.ds(0, DK)] * lat_ref[pl.ds(b * CS, CS), :].astype(F32)
    for j in range(PIECES):
        w = piece_width(j)
        part[pl.ds(j, CS, stride=SLOT), pl.ds(0, w)] = weight[:, j * LANES : j * LANES + w]
    to_owners(lambda peer: part_copy(peer).start())

    def merge(k):
        to_sibling(k, 1).wait_recv()
        wing[segment(2 * k), :] = (seg_grad(2 * k) + srecv[k].astype(F32)).astype(BF16)
        to_source(k).start()

    for k in range(reach, 0, -1):
        if k < reach:
            pl.when(base >= 2 * k)(lambda k=k: merge(k))
        else:
            pl.when((parity == 1) & (base >= 2 * k))(lambda k=k: merge(k))

    @if_owner
    def _():
        precv[me] = part[pl.ds(pl.multiple_of(me * per, per), per), :]
        each(count, me, lambda peer: part_wait(peer).wait_recv())
        pout[pl.ds(pl.multiple_of(me * per, per), per), :] = jnp.sum(precv[...], axis=0)
        each(count, me, lambda peer: out_copy(peer).start())

    for m in range(H // 2):
        even = pl.ds(m * tok, tok)
        odd = pl.ds(half + m * tok, tok)
        qg_buf[:, pl.ds(m * pair, DL)] = dq[even, pl.ds(0, DL)].astype(BF16)
        qg_buf[:, pl.ds(m * pair + DL, LANES)] = (
            dq[even, pl.ds(DL, LANES)] + dq[odd, pl.ds(0, LANES)]
        ).astype(BF16)
        qg_buf[:, pl.ds(m * pair + WIDE, DL)] = dq[odd, pl.ds(LANES, DL)].astype(BF16)
    save_qg = pltpu.make_async_copy(qg_buf, qg_ref, save_sem.at[1])
    save_qg.start()

    own = seg_grad(0)
    for b in range(cl):
        rows = pl.ds(b * CS, CS)
        lg_ref[rows, :] = own[b * CS : (b + 1) * CS] + cw_ref[...] * cgrad[pl.ds(b, 1), pl.ds(0, DK)]

    @pl.when(parity == 0)
    def _():
        to_sibling(0, 1).wait_recv()
        lg_ref[...] += srecv[0].astype(F32)

    for k in range(1, reach + 1):

        @pl.when(base + 2 * k < n)
        def _(k=k):
            to_source(k).wait_recv()
            lg_ref[...] += wrecv[k - 1].astype(F32)

    to_owners(lambda peer: out_wait(peer).wait_recv())
    for j in range(PIECES):
        w = piece_width(j)
        wg_ref[:, pl.ds(j * LANES, w)] = pout[pl.ds(j, CS, stride=SLOT), :][:, :w]

    save_att.wait()
    save_qg.wait()
    each(n, seq, lambda peer: comp_send(peer).wait_send())
    each(n, seq, lambda peer: sum_send(peer).wait_send())
    for k in range(1, reach + 1):
        pl.when(base + 2 * k < n)(lambda k=k: win_copy(k).wait_send())
        pl.when(base >= 2 * k)(lambda k=k: to_source(k).wait_send())
    forwarded(lambda k, d, unused: pass_on(k, d).wait_send())
    back(lambda k, d, unused: to_sibling(k, d).wait_send())
    to_owners(lambda peer: part_copy(peer).wait_send())
    if_owner(lambda: each(count, me, lambda peer: out_copy(peer).wait_send()))


def body(n, groups, queries, latents, cotangent, comp_weight, sel_idx, sel_count):
    tok = latents.shape[1]
    hop = (WIN + tok - 1) // tok
    assert hop % 2 == 0 and n % 2 == 0
    lead = hop * tok
    cl = tok // CS
    pr = round_up(cl * PIECES, 16)
    nk = round_up(n * SLOT, LANES) + round_up(lead + tok, LANES)
    count = n * groups
    owners = min(CS, count)
    per = CS // owners * SLOT
    dma = pltpu.SemaphoreType.DMA
    reach = hop // 2
    any_spec = pl.BlockSpec(memory_space=pl.ANY)
    vmem_spec = pl.BlockSpec(memory_space=pltpu.VMEM)
    att, qg, lat_grad, weight_grad = pl.pallas_call(
        functools.partial(kernel, n, groups, hop, tok, cl, owners),
        out_shape=(
            jax.ShapeDtypeStruct((tok, H * DL), BF16),
            jax.ShapeDtypeStruct((tok, H * DK), BF16),
            jax.ShapeDtypeStruct((tok, DK), F32),
            jax.ShapeDtypeStruct((CS, DK), F32),
        ),
        in_specs=[
            any_spec,
            any_spec,
            vmem_spec,
            vmem_spec,
            vmem_spec,
            pl.BlockSpec(memory_space=pltpu.SMEM),
        ],
        out_specs=(any_spec, any_spec, vmem_spec, vmem_spec),
        scratch_shapes=[
            pltpu.VMEM((H * tok, WIDE), BF16),
            pltpu.VMEM((H * tok, DL), BF16),
            pltpu.VMEM((lead, DK), BF16),
            pltpu.VMEM((n, pr, LANES), BF16),
            pltpu.VMEM((pr, LANES), F32),
            pltpu.VMEM((2, nk, WIDE), BF16),
            pltpu.VMEM((nk, WIDE), F32),
            pltpu.VMEM((tok, nk), F32),
            pltpu.VMEM((H * tok, nk), BF16),
            pltpu.VMEM((H * tok, nk), BF16),
            pltpu.VMEM((H * tok, WIDE), F32),
            pltpu.VMEM((tok, H * DL), BF16),
            pltpu.VMEM((tok, H * DK), BF16),
            pltpu.VMEM((n, pr, LANES), F32),
            pltpu.VMEM((n, pr, LANES), BF16),
            pltpu.VMEM((n, pr, LANES), BF16),
            pltpu.VMEM((SLOT, WIDE), F32),
            pltpu.VMEM((CS * SLOT, LANES), F32),
            pltpu.VMEM((count, per, LANES), F32),
            pltpu.VMEM((CS * SLOT, LANES), F32),
            pltpu.VMEM((lead, DK), BF16),
            pltpu.VMEM((reach + 1, tok, DK), BF16),
            pltpu.VMEM((reach, tok, DK), BF16),
            dma((2 * H,)),
            dma((2,)),
            dma((n,)),
            dma((n,)),
            dma((reach + 1,)),
            dma((reach + 1,)),
            dma((reach + 1,)),
            dma((hop + 1,)),
            dma((n,)),
            dma((n,)),
            dma((reach + 1,)),
            dma((reach + 1,)),
            dma((reach + 1,)),
            dma((reach + 1,)),
            dma((count,)),
            dma((count,)),
            dma((count,)),
            dma((count,)),
        ],
        compiler_params=pltpu.CompilerParams(
            collective_id=0, has_side_effects=True, vmem_limit_bytes=56 * 2**20
        ),
    )(queries[0], cotangent[0], latents[0], comp_weight, sel_idx[0], sel_count)
    return (att[None], qg[None], lat_grad[None], weight_grad)


def solution(mesh):
    in_specs = (
        P("grp", "seq", None),
        P("grp", "seq", None),
        P("grp", "seq", None),
        P(),
        P("grp", "seq", None),
        P("grp", "seq"),
    )
    out_specs = (P("grp", "seq", None), P("grp", "seq", None), P("grp", "seq", None), P())
    return jax.shard_map(
        functools.partial(body, mesh.shape["seq"], mesh.shape["grp"]),
        mesh=mesh,
        in_specs=in_specs,
        out_specs=out_specs,
        check_vma=False,
    )
```

time: 76.8 us -> 56.9 us (0.74)
  Pallas kernels: 70.8 us -> 48.4 us
  local copies, waits for them, and re-layouts: 5.08 us -> 7.59 us
    pallas_call x3 -> x1, Pallas kernels: 70.8 us -> 48.4 us  [body(): pl.pallas_call(functools.partial(kernel, n, groups, hop, tok, cl, owners)...]
    unnamed x3 -> x9, local copies, waits for them, and re-layouts: 5.08 us -> 7.59 us
where the time goes in v2:
time: 56.9 us; the launch traced here: 56.6 us
  Pallas kernels  48.4 us (85%)
  local copies, waits for them, and re-layouts  7.59 us (13%)
  between operations  0.64 us (1%)
    pallas_call x1, Pallas kernels, body(): pl.pallas_call(functools.partial(kernel, n, groups, hop, tok, cl, owners)...  48.4 us
    unnamed x9, local copies, waits for them, and re-layouts  7.59 us

profile of v2, /device:TPU:0, one launch (start us, length us, event | category | flops | bytes accessed | tf_op | source)
XLA Modules:
  0.0 56.6 jit_solution(18165580894865091174)
XLA Ops:
  0.6 1.7 %copy.10 = bf16[1,128,576]{2,1,0:T(8,128)(2,1)} copy(bf16[1,128,576]{1,2,0:T(8,128)(2,1)} %param.7) | data formatting | bytes 294912 | tf_op args[1]
  2.3 48.4 %shard_map.93 = (bf16[128,4096]{1,0:T(8,128)(2,1)}, bf16[128,4608]{1,0:T(8,128)(2,1)}, f32[128,576]{1,0:T(8,128)}, f32[32,576]{1,0:T(8,128)}) custom-call(bf16[128,4608]{1,0:T(8,128)(2,1)} %bitcast.7, bf16[128,4096]{1,0:T(8,128)(2,1)} %bitcast.9, bf16[128,576]{1,0:T(8,128)(2,1)} %bitcast.11, f32[32,576]{1,0:T(8,128)} %cw_ref.1, s32[2,64]{1,0:T(2,128)} %bitcast.13, ...), custom_call_target="tpu_custom_call" | custom-call | tf_op jit(solution)/shard_map/pallas_call | solution.py:449
  50.8 1.8 %copy.11 = f32[1,128,576]{1,2,0:T(8,128)} copy(f32[1,128,576]{2,1,0:T(8,128)} %bitcast.12) | data formatting | bytes 589824
  52.6 0.0 copy-start
  52.6 2.4 %copy.15 = bf16[1,128,4096]{2,1,0:T(8,128)(2,1)} copy(bf16[1,128,4096]{2,1,0:T(8,128)(2,1)} %bitcast.10) | data formatting | bytes 2097152
  55.0 0.0 copy-done
  55.0 0.0 copy-start.1
  55.0 1.0 %copy.16 = bf16[1,128,4608]{2,1,0:T(8,128)(2,1)} copy(bf16[1,128,4608]{2,1,0:T(8,128)(2,1)S(1)} %bitcast.8) | data formatting | bytes 2359296
  56.0 0.0 copy-done.1
  56.0 0.6 %copy.17 = f32[32,576]{1,0:T(8,128)} copy(f32[32,576]{1,0:T(8,128)S(1)} %copy-done.1) | data formatting | bytes 147456
Async XLA Ops:
  52.6 2.4 %copy-start = (bf16[128,4608]{1,0:T(8,128)(2,1)S(1)}, bf16[128,4608]{1,0:T(8,128)(2,1)}, u32[]{:S(2)}) copy-start(bf16[128,4608]{1,0:T(8,128)(2,1)} %get-tuple-element.9) | copy-start | bytes 3538948
  55.0 1.0 %copy-start.1 = (f32[32,576]{1,0:T(8,128)S(1)}, f32[32,576]{1,0:T(8,128)}, u32[]{:S(2)}) copy-start(f32[32,576]{1,0:T(8,128)} %get-tuple-element.23) | copy-start | bytes 221188

commit v3 on v2

--- a/solution.py
+++ b/solution.py
@@ -19,6 +19,7 @@
 PIECES = WIDE // LANES
 SLOT = 8
 MASKED = -1e30
+UNROLL = 32
 
 MESH = pl.DeviceIdType.MESH
 BF16 = jnp.bfloat16
@@ -47,8 +48,13 @@
 
 
 def each(size, base, work):
+    if size <= UNROLL:
+        for k in range(1, size):
+            work(lax.rem(base + k, size))
+        return
+
     def one(k, c):
-        work((base + k) % size)
+        work(lax.rem(base + k, size))
         return c
 
     lax.fori_loop(1, size, one, 0)
@@ -56,9 +62,9 @@
 
 def kernel(
     n, groups, hop, tok, cl, owners,
-    q_ref, cot_ref, lat_ref, cw_ref, idx_ref, cnt_ref,
-    att_ref, qg_ref, lg_ref, wg_ref,
-    qq, cc, win, comp, tmp, kk, kf, bias, ds_ref, pp, dq, att_buf, qg_buf,
+    q_ref, cot_ref, lat_t_ref, cw_ref, idx_ref, cnt_ref,
+    att_ref, qg_ref, lg_t_ref, wg_ref,
+    lat_ref, lg_ref, qq, cc, win, comp, tmp, kk, kf, bias, ds_ref, pp, dq, att_buf, qg_buf,
     pack, cg, crecv_buf, cgrad, part, precv, pout, wing, srecv, wrecv,
     load_sem, save_sem,
     gc_send, gc_recv, gw_send, gw_recv, gs_send, gs_recv,
@@ -82,13 +88,16 @@
     reach = hop // 2
 
     def where(peer):
-        return (peer // n, peer % n)
+        return (lax.div(peer, n), lax.rem(peer, n))
 
     def remote(src, dst, send, recv, device):
         return pltpu.make_async_remote_copy(
             src_ref=src, dst_ref=dst, send_sem=send, recv_sem=recv,
             device_id=device, device_id_type=MESH,
         )
+
+    def wait_all(ref, sem):
+        remote(ref, ref, sem, sem, (grp, sibling)).wait_recv()
 
     def segment(d):
         return pl.ds((hop - d) * tok, tok)
@@ -119,6 +128,7 @@
     for load in loads:
         load.start()
 
+    lat_ref[...] = lat_t_ref[...].astype(F32).T.astype(BF16)
     tmp[...] = jnp.zeros_like(tmp)
     for b in range(cl):
         block = lat_ref[pl.ds(b * CS, CS), :].astype(F32) * cw_ref[...]
@@ -130,10 +140,7 @@
     pl.semaphore_wait(barrier, count - 1)
 
     def comp_send(peer):
-        return remote(comp.at[seq], comp.at[seq], gc_send.at[peer], gc_recv.at[seq], (grp, peer))
-
-    def comp_wait(peer):
-        return remote(comp.at[peer], comp.at[peer], gc_send.at[peer], gc_recv.at[peer], (grp, peer))
+        return remote(comp.at[seq], comp.at[seq], gc_send, gc_recv, (grp, peer))
 
     def win_copy(k):
         return remote(
@@ -198,7 +205,7 @@
                 pl.when(parity == 0)(lambda: pass_on(k, 2 * k + 1).start())
             pl.when(parity == 1)(lambda: pass_on(k, 2 * k - 1).start())
 
-    each(n, seq, lambda peer: comp_wait(peer).wait_recv())
+    wait_all(comp.at[pl.ds(0, n - 1)], gc_recv)
 
     def unpack(o, c):
         packed = comp[o].astype(F32)
@@ -264,12 +271,7 @@
         return kf[pl.ds(cp + (hop - d) * tok, tok), pl.ds(0, DK)]
 
     def sum_send(peer):
-        return remote(cg.at[peer], crecv_buf.at[seq], rc_send.at[peer], rc_recv.at[seq], (grp, peer))
-
-    def sum_wait(peer):
-        return remote(
-            cg.at[peer], crecv_buf.at[peer], rc_send.at[peer], rc_recv.at[peer], (grp, peer)
-        )
+        return remote(cg.at[peer], crecv_buf.at[seq], rc_send, rc_recv, (grp, peer))
 
     def to_sibling(k, d):
         return remote(
@@ -284,22 +286,19 @@
 
     def part_copy(peer):
         return remote(
-            part.at[pl.ds(peer * per, per)], precv.at[me], p_send.at[peer], p_recv.at[me],
-            where(peer),
-        )
-
-    def part_wait(peer):
-        return remote(
-            part.at[pl.ds(0, per)], precv.at[peer], p_send.at[0], p_recv.at[peer], where(peer)
+            part.at[pl.ds(peer * per, per)], precv.at[me], p_send, p_recv, where(peer)
         )
 
     def out_copy(peer):
         rows = pl.ds(me * per, per)
-        return remote(pout.at[rows], pout.at[rows], o_send.at[peer], o_recv.at[me], where(peer))
-
-    def out_wait(peer):
-        rows = pl.ds(peer * per, per)
-        return remote(pout.at[rows], pout.at[rows], o_send.at[peer], o_recv.at[peer], where(peer))
+        return remote(pout.at[rows], pout.at[rows], o_send, o_recv, where(peer))
+
+    def wait_owners(ref, sem):
+        if owners == count:
+            wait_all(ref.at[pl.ds(0, (owners - 1) * per)], sem)
+        else:
+            pl.when(me < owners)(lambda: wait_all(ref.at[pl.ds(0, (owners - 1) * per)], sem))
+            pl.when(me >= owners)(lambda: wait_all(ref.at[pl.ds(0, owners * per)], sem))
 
     def to_owners(work):
         def one(peer):
@@ -333,11 +332,7 @@
     crecv_buf[seq] = cg[seq]
     each(n, seq, lambda peer: sum_send(peer).start())
 
-    while done < nk:
-        key_pass(done)
-        done += 256
-
-    def send_sibling(k, d, unused):
+    def send_sibling(k, d):
         wing[segment(d), :] = seg_grad(d).astype(BF16)
         to_sibling(k, d).start()
 
@@ -348,14 +343,30 @@
             if k < reach:
                 pl.when((parity == 1) & (base >= 2 * k))(lambda k=k: work(k, 2 * k + 1, False))
 
-    back(send_sibling)
-
-    @pl.when((parity == 0) & (base >= hop))
-    def _():
-        wing[segment(hop), :] = seg_grad(hop).astype(BF16)
-        to_source(reach).start()
-
-    each(n, seq, lambda peer: sum_wait(peer).wait_recv())
+    def ship(d):
+        if d == hop:
+
+            @pl.when((parity == 0) & (base >= hop))
+            def _():
+                wing[segment(hop), :] = seg_grad(hop).astype(BF16)
+                to_source(reach).start()
+
+        elif d % 2 == 1:
+            k = (d + 1) // 2
+            pl.when((parity == 0) & (base >= 2 * k))(lambda: send_sibling(k, d))
+            pl.when((parity == 1) & (base >= 2 * k - 2))(lambda: send_sibling(k - 1, d))
+
+    ready = hop
+    while True:
+        while ready > 0 and cp + (hop - ready + 1) * tok <= done:
+            ship(ready)
+            ready -= 1
+        if done >= nk:
+            break
+        key_pass(done)
+        done += 256
+
+    wait_all(crecv_buf.at[pl.ds(0, n - 1)], rc_recv)
     total = jnp.sum(crecv_buf[...].astype(F32), axis=0)
     for j in range(PIECES):
         cgrad[pl.ds(0, cl), pl.ds(j * LANES, LANES)] = total[j * cl : (j + 1) * cl, :]
@@ -381,7 +392,7 @@
     @if_owner
     def _():
         precv[me] = part[pl.ds(pl.multiple_of(me * per, per), per), :]
-        each(count, me, lambda peer: part_wait(peer).wait_recv())
+        wait_all(precv.at[pl.ds(0, count - 1)], p_recv)
         pout[pl.ds(pl.multiple_of(me * per, per), per), :] = jnp.sum(precv[...], axis=0)
         each(count, me, lambda peer: out_copy(peer).start())
 
@@ -413,22 +424,23 @@
             to_source(k).wait_recv()
             lg_ref[...] += wrecv[k - 1].astype(F32)
 
-    to_owners(lambda peer: out_wait(peer).wait_recv())
+    lg_t_ref[...] = lg_ref[...].T
+    wait_owners(pout, o_recv)
     for j in range(PIECES):
         w = piece_width(j)
         wg_ref[:, pl.ds(j * LANES, w)] = pout[pl.ds(j, CS, stride=SLOT), :][:, :w]
 
     save_att.wait()
     save_qg.wait()
-    each(n, seq, lambda peer: comp_send(peer).wait_send())
-    each(n, seq, lambda peer: sum_send(peer).wait_send())
+    wait_all(comp.at[pl.ds(0, n - 1)], gc_send)
+    wait_all(cg.at[pl.ds(0, n - 1)], rc_send)
     for k in range(1, reach + 1):
         pl.when(base + 2 * k < n)(lambda k=k: win_copy(k).wait_send())
         pl.when(base >= 2 * k)(lambda k=k: to_source(k).wait_send())
     forwarded(lambda k, d, unused: pass_on(k, d).wait_send())
     back(lambda k, d, unused: to_sibling(k, d).wait_send())
-    to_owners(lambda peer: part_copy(peer).wait_send())
-    if_owner(lambda: each(count, me, lambda peer: out_copy(peer).wait_send()))
+    wait_owners(part, p_send)
+    if_owner(lambda: wait_all(precv.at[pl.ds(0, count - 1)], o_send))
 
 
 def body(n, groups, queries, latents, cotangent, comp_weight, sel_idx, sel_count):
@@ -451,7 +463,7 @@
         out_shape=(
             jax.ShapeDtypeStruct((tok, H * DL), BF16),
             jax.ShapeDtypeStruct((tok, H * DK), BF16),
-            jax.ShapeDtypeStruct((tok, DK), F32),
+            jax.ShapeDtypeStruct((DK, tok), F32),
             jax.ShapeDtypeStruct((CS, DK), F32),
         ),
         in_specs=[
@@ -464,6 +476,8 @@
         ],
         out_specs=(any_spec, any_spec, vmem_spec, vmem_spec),
         scratch_shapes=[
+            pltpu.VMEM((tok, DK), BF16),
+            pltpu.VMEM((tok, DK), F32),
             pltpu.VMEM((H * tok, WIDE), BF16),
             pltpu.VMEM((H * tok, DL), BF16),
             pltpu.VMEM((lead, DK), BF16),
@@ -489,28 +503,28 @@
             pltpu.VMEM((reach, tok, DK), BF16),
             dma((2 * H,)),
             dma((2,)),
-            dma((n,)),
-            dma((n,)),
+            dma,
+            dma,
             dma((reach + 1,)),
             dma((reach + 1,)),
             dma((reach + 1,)),
             dma((hop + 1,)),
-            dma((n,)),
-            dma((n,)),
-            dma((reach + 1,)),
-            dma((reach + 1,)),
-            dma((reach + 1,)),
-            dma((reach + 1,)),
-            dma((count,)),
-            dma((count,)),
-            dma((count,)),
-            dma((count,)),
+            dma,
+            dma,
+            dma((reach + 1,)),
+            dma((reach + 1,)),
+            dma((reach + 1,)),
+            dma((reach + 1,)),
+            dma,
+            dma,
+            dma,
+            dma,
         ],
         compiler_params=pltpu.CompilerParams(
             collective_id=0, has_side_effects=True, vmem_limit_bytes=56 * 2**20
         ),
-    )(queries[0], cotangent[0], latents[0], comp_weight, sel_idx[0], sel_count)
-    return (att[None], qg[None], lat_grad[None], weight_grad)
+    )(queries[0], cotangent[0], jnp.swapaxes(latents[0], 0, 1), comp_weight, sel_idx[0], sel_count)
+    return (att[None], qg[None], jnp.swapaxes(lat_grad, 0, 1)[None], weight_grad)
 
 
 def solution(mesh):

time: 56.9 us -> 51 us (0.90)
  Pallas kernels: 48.4 us -> 45.3 us
  local copies, waits for them, and re-layouts: 7.59 us -> 4.86 us
    pallas_call x1, Pallas kernels: 48.4 us -> 45.3 us  [body(): pl.pallas_call(functools.partial(kernel, n, groups, hop, tok, cl, owners)...]
    unnamed x9 -> x10, local copies, waits for them, and re-layouts: 7.59 us -> 4.86 us
where the time goes in v3:
time: 51 us; the launch traced here: 50.8 us
  Pallas kernels  45.3 us (89%)
  local copies, waits for them, and re-layouts  4.86 us (10%)
  between operations  0.65 us (1%)
    pallas_call x1, Pallas kernels, body(): pl.pallas_call(functools.partial(kernel, n, groups, hop, tok, cl, owners)...  45.3 us
    unnamed x10, local copies, waits for them, and re-layouts  4.86 us

profile of v3, /device:TPU:0, one launch (start us, length us, event | category | flops | bytes accessed | tf_op | source)
XLA Modules:
  0.0 50.8 jit_solution(2537842139876131918)
XLA Ops:
  0.6 45.3 %shard_map.93 = (bf16[128,4096]{1,0:T(8,128)(2,1)}, bf16[128,4608]{1,0:T(8,128)(2,1)}, f32[576,128]{1,0:T(8,128)}, f32[32,576]{1,0:T(8,128)}) custom-call(bf16[128,4608]{1,0:T(8,128)(2,1)} %bitcast.11, bf16[128,4096]{1,0:T(8,128)(2,1)} %bitcast.13, bf16[576,128]{1,0:T(8,128)(2,1)} %bitcast.16, f32[32,576]{1,0:T(8,128)} %cw_ref.1, s32[2,64]{1,0:T(2,128)} %bitcast.17, ...), custom_call_target="tpu_custom_call" | custom-call | tf_op jit(solution)/shard_map/pallas_call | solution.py:461
  46.0 0.0 copy-start
  46.0 2.4 %copy.14 = bf16[1,128,4096]{2,1,0:T(8,128)(2,1)} copy(bf16[1,128,4096]{2,1,0:T(8,128)(2,1)} %bitcast.14) | data formatting | bytes 2097152
  48.4 0.0 copy-done
  48.4 0.0 copy-start.1
  48.4 0.0 copy-start.2
  48.4 1.0 %copy.15 = bf16[1,128,4608]{2,1,0:T(8,128)(2,1)} copy(bf16[1,128,4608]{2,1,0:T(8,128)(2,1)S(1)} %bitcast.12) | data formatting | bytes 2359296
  49.4 0.1 copy-done.1
  49.5 0.7 %copy.16 = f32[1,128,576]{1,2,0:T(8,128)} copy(f32[1,128,576]{1,2,0:T(8,128)S(1)} %bitcast.15) | data formatting | bytes 589824
  50.2 0.0 copy-done.2
  50.2 0.6 %copy.17 = f32[32,576]{1,0:T(8,128)} copy(f32[32,576]{1,0:T(8,128)S(1)} %copy-done.2) | data formatting | bytes 147456
Async XLA Ops:
  46.0 2.4 %copy-start = (bf16[128,4608]{1,0:T(8,128)(2,1)S(1)}, bf16[128,4608]{1,0:T(8,128)(2,1)}, u32[]{:S(2)}) copy-start(bf16[128,4608]{1,0:T(8,128)(2,1)} %get-tuple-element.9) | copy-start | bytes 3538948
  48.4 1.1 %copy-start.1 = (f32[576,128]{1,0:T(8,128)S(1)}, f32[576,128]{1,0:T(8,128)}, u32[]{:S(2)}) copy-start(f32[576,128]{1,0:T(8,128)} %get-tuple-element.10) | copy-start | bytes 884740
  48.4 1.8 %copy-start.2 = (f32[32,576]{1,0:T(8,128)S(1)}, f32[32,576]{1,0:T(8,128)}, u32[]{:S(2)}) copy-start(f32[32,576]{1,0:T(8,128)} %get-tuple-element.19) | copy-start | bytes 221188

commit v4 on v3

--- a/solution.py
+++ b/solution.py
@@ -20,6 +20,7 @@
 SLOT = 8
 MASKED = -1e30
 UNROLL = 32
+INNER = 4
 
 MESH = pl.DeviceIdType.MESH
 BF16 = jnp.bfloat16
@@ -61,24 +62,27 @@
 
 
 def kernel(
-    n, groups, hop, tok, cl, owners,
+    n, groups, hop, tok, cl, inner,
     q_ref, cot_ref, lat_t_ref, cw_ref, idx_ref, cnt_ref,
     att_ref, qg_ref, lg_t_ref, wg_ref,
     lat_ref, lg_ref, qq, cc, win, comp, tmp, kk, kf, bias, ds_ref, pp, dq, att_buf, qg_buf,
-    pack, cg, crecv_buf, cgrad, part, precv, pout, wing, srecv, wrecv,
+    pack, cg, crecv_buf, cgrad, part, precv, lines, pout, wing, srecv, wrecv,
     load_sem, save_sem,
     gc_send, gc_recv, gw_send, gw_recv, gs_send, gs_recv,
     rc_send, rc_recv, rs_send, rs_recv, rw_send, rw_recv,
-    p_send, p_recv, o_send, o_recv,
+    p_send, p_recv, l_send, l_recv, o_send, o_recv,
 ):
     seq = lax.axis_index("seq")
     grp = lax.axis_index("grp")
-    count = n * groups
-    me = grp * n + seq
+    outer = n // inner
+    plane = groups * inner
+    depth = seq // inner
+    spot = seq % inner
+    rank = grp * inner + spot
     parity = seq % 2
     base = seq - parity
     sibling = base + 1 - parity
-    per = CS // owners * SLOT
+    own_rows = CS // plane
     nk = bias.shape[1]
     lead = hop * tok
     ext = lead + tok
@@ -87,8 +91,11 @@
     pair = 2 * DK
     reach = hop // 2
 
-    def where(peer):
-        return (lax.div(peer, n), lax.rem(peer, n))
+    def in_plane(peer):
+        return (lax.div(peer, inner), depth * inner + lax.rem(peer, inner))
+
+    def along(peer):
+        return (grp, peer * inner + spot)
 
     def remote(src, dst, send, recv, device):
         return pltpu.make_async_remote_copy(
@@ -103,12 +110,14 @@
         return pl.ds((hop - d) * tok, tok)
 
     barrier = pltpu.get_barrier_semaphore()
-    each(
-        count, me,
-        lambda peer: pl.semaphore_signal(
-            barrier, inc=1, device_id=where(peer), device_id_type=MESH
-        ),
-    )
+
+    def greet(device):
+        pl.semaphore_signal(barrier, inc=1, device_id=device, device_id_type=MESH)
+
+    each(n, seq, lambda peer: greet((grp, peer)))
+    for g in range(1, groups):
+        for i in range(inner):
+            greet((lax.rem(grp + g, groups), depth * inner + i))
 
     loads = []
     for m in range(H // 2):
@@ -137,7 +146,7 @@
             w = piece_width(j)
             tmp[pl.ds(j * cl + b, 1), pl.ds(0, w)] = row[:, j * LANES : j * LANES + w]
     comp[seq] = tmp[...].astype(BF16)
-    pl.semaphore_wait(barrier, count - 1)
+    pl.semaphore_wait(barrier, n - 1 + (groups - 1) * inner)
 
     def comp_send(peer):
         return remote(comp.at[seq], comp.at[seq], gc_send, gc_recv, (grp, peer))
@@ -189,10 +198,18 @@
     ok = (col > row + shift) & (col <= row + lead) & (col - lead + seq * tok >= 0)
     bias[:, pl.ds(cp, wide)] = jnp.where(ok, 0.0, MASKED)
     kf[pl.ds(0, cp), :] = jnp.zeros((cp, WIDE), F32)
-    kf[pl.ds(cp, ext), pl.ds(DL, LANES)] = jnp.zeros((ext, LANES), F32)
-    kf[pl.ds(cp + lead, tok), pl.ds(0, DK)] = lat_ref[...].astype(F32)
     if nk > cp + ext:
-        kf[pl.ds(cp + ext, nk - cp - ext), :] = jnp.zeros((nk - cp - ext, WIDE), F32)
+        kk[:, pl.ds(cp + ext, nk - cp - ext), :] = jnp.zeros((2, nk - cp - ext, WIDE), BF16)
+
+    def lay_out(d, value):
+        rows = pl.ds(cp + (hop - d) * tok, tok)
+        padded = jnp.concatenate(
+            [value.astype(F32), jnp.zeros((tok, WIDE - DK), F32)], axis=1
+        )
+        kk[0, rows, :] = padded.astype(BF16)
+        kk[1, rows, :] = pltpu.roll(padded, DR, 1).astype(BF16)
+
+    lay_out(0, lat_ref[...])
     pack[...] = jnp.zeros_like(pack)
     part[...] = jnp.zeros_like(part)
 
@@ -205,6 +222,8 @@
                 pl.when(parity == 0)(lambda: pass_on(k, 2 * k + 1).start())
             pl.when(parity == 1)(lambda: pass_on(k, 2 * k - 1).start())
 
+    for k in range(1, reach + 1):
+        lay_out(2 * k, win[segment(2 * k), :])
     wait_all(comp.at[pl.ds(0, n - 1)], gc_recv)
 
     def unpack(o, c):
@@ -216,6 +235,8 @@
         return c
 
     lax.fori_loop(0, n, unpack, 0)
+    kk[0, pl.ds(0, cp), :] = kf[pl.ds(0, cp), :].astype(BF16)
+    kk[1, pl.ds(0, cp), :] = pltpu.roll(kf[pl.ds(0, cp), :], DR, 1).astype(BF16)
 
     def sibling_arrival(k, d):
         pass_on(k, d).wait_recv()
@@ -225,9 +246,8 @@
             pl.when((parity == 1) & (base >= 2 * k))(lambda k=k: sibling_arrival(k, 2 * k + 1))
         if k > 0:
             pl.when((parity == 0) & (base >= 2 * k))(lambda k=k: sibling_arrival(k, 2 * k - 1))
-    kf[pl.ds(cp, lead), pl.ds(0, DK)] = win[...].astype(F32)
-    kk[0] = kf[...].astype(BF16)
-    kk[1] = pltpu.roll(kf[...], DR, 1).astype(BF16)
+    for d in range(1, hop + 1, 2):
+        lay_out(d, win[segment(d), :])
     for load in loads:
         load.wait()
 
@@ -285,35 +305,13 @@
         )
 
     def part_copy(peer):
-        return remote(
-            part.at[pl.ds(peer * per, per)], precv.at[me], p_send, p_recv, where(peer)
-        )
+        return remote(part.at[peer], precv.at[rank], p_send, p_recv, in_plane(peer))
+
+    def line_copy(peer):
+        return remote(lines.at[depth], lines.at[depth], l_send, l_recv, along(peer))
 
     def out_copy(peer):
-        rows = pl.ds(me * per, per)
-        return remote(pout.at[rows], pout.at[rows], o_send, o_recv, where(peer))
-
-    def wait_owners(ref, sem):
-        if owners == count:
-            wait_all(ref.at[pl.ds(0, (owners - 1) * per)], sem)
-        else:
-            pl.when(me < owners)(lambda: wait_all(ref.at[pl.ds(0, (owners - 1) * per)], sem))
-            pl.when(me >= owners)(lambda: wait_all(ref.at[pl.ds(0, owners * per)], sem))
-
-    def to_owners(work):
-        def one(peer):
-            if owners == count:
-                work(peer)
-            else:
-                pl.when(peer < owners)(lambda: work(peer))
-
-        each(count, me, one)
-
-    def if_owner(work):
-        if owners == count:
-            work()
-        else:
-            pl.when(me < owners)(work)
+        return remote(pout.at[rank], pout.at[rank], o_send, o_recv, in_plane(peer))
 
     done = 0
     while done < cp:
@@ -373,10 +371,18 @@
     weight = jnp.zeros((CS, DK), F32)
     for b in range(cl):
         weight = weight + cgrad[pl.ds(b, 1), pl.ds(0, DK)] * lat_ref[pl.ds(b * CS, CS), :].astype(F32)
-    for j in range(PIECES):
-        w = piece_width(j)
-        part[pl.ds(j, CS, stride=SLOT), pl.ds(0, w)] = weight[:, j * LANES : j * LANES + w]
-    to_owners(lambda peer: part_copy(peer).start())
+    for o in range(plane):
+        for j in range(PIECES):
+            w = piece_width(j)
+            part[o, pl.ds(j * own_rows, own_rows), pl.ds(0, w)] = weight[
+                o * own_rows : (o + 1) * own_rows, j * LANES : j * LANES + w
+            ]
+    each(plane, rank, lambda peer: part_copy(peer).start())
+    precv[rank] = part[rank]
+
+    wait_all(precv.at[pl.ds(0, plane - 1)], p_recv)
+    lines[depth] = jnp.sum(precv[...], axis=0)
+    each(outer, depth, lambda peer: line_copy(peer).start())
 
     def merge(k):
         to_sibling(k, 1).wait_recv()
@@ -389,12 +395,9 @@
         else:
             pl.when((parity == 1) & (base >= 2 * k))(lambda k=k: merge(k))
 
-    @if_owner
-    def _():
-        precv[me] = part[pl.ds(pl.multiple_of(me * per, per), per), :]
-        wait_all(precv.at[pl.ds(0, count - 1)], p_recv)
-        pout[pl.ds(pl.multiple_of(me * per, per), per), :] = jnp.sum(precv[...], axis=0)
-        each(count, me, lambda peer: out_copy(peer).start())
+    wait_all(lines.at[pl.ds(0, outer - 1)], l_recv)
+    pout[rank] = jnp.sum(lines[...], axis=0)
+    each(plane, rank, lambda peer: out_copy(peer).start())
 
     for m in range(H // 2):
         even = pl.ds(m * tok, tok)
@@ -425,10 +428,13 @@
             lg_ref[...] += wrecv[k - 1].astype(F32)
 
     lg_t_ref[...] = lg_ref[...].T
-    wait_owners(pout, o_recv)
-    for j in range(PIECES):
-        w = piece_width(j)
-        wg_ref[:, pl.ds(j * LANES, w)] = pout[pl.ds(j, CS, stride=SLOT), :][:, :w]
+    wait_all(pout.at[pl.ds(0, plane - 1)], o_recv)
+    for o in range(plane):
+        for j in range(PIECES):
+            w = piece_width(j)
+            wg_ref[pl.ds(o * own_rows, own_rows), pl.ds(j * LANES, w)] = pout[
+                o, pl.ds(j * own_rows, own_rows), pl.ds(0, w)
+            ]
 
     save_att.wait()
     save_qg.wait()
@@ -439,8 +445,9 @@
         pl.when(base >= 2 * k)(lambda k=k: to_source(k).wait_send())
     forwarded(lambda k, d, unused: pass_on(k, d).wait_send())
     back(lambda k, d, unused: to_sibling(k, d).wait_send())
-    wait_owners(part, p_send)
-    if_owner(lambda: wait_all(precv.at[pl.ds(0, count - 1)], o_send))
+    wait_all(part.at[pl.ds(0, plane - 1)], p_send)
+    wait_all(lines.at[pl.ds(0, outer - 1)], l_send)
+    wait_all(pout.at[pl.ds(0, plane - 1)], o_send)
 
 
 def body(n, groups, queries, latents, cotangent, comp_weight, sel_idx, sel_count):
@@ -451,15 +458,17 @@
     cl = tok // CS
     pr = round_up(cl * PIECES, 16)
     nk = round_up(n * SLOT, LANES) + round_up(lead + tok, LANES)
-    count = n * groups
-    owners = min(CS, count)
-    per = CS // owners * SLOT
+    inner = INNER
+    plane = groups * inner
+    assert n % inner == 0 and CS % plane == 0
+    own_pack = round_up(CS // plane * PIECES, SLOT)
     dma = pltpu.SemaphoreType.DMA
     reach = hop // 2
     any_spec = pl.BlockSpec(memory_space=pl.ANY)
+    hbm_spec = pl.BlockSpec(memory_space=pltpu.HBM)
     vmem_spec = pl.BlockSpec(memory_space=pltpu.VMEM)
     att, qg, lat_grad, weight_grad = pl.pallas_call(
-        functools.partial(kernel, n, groups, hop, tok, cl, owners),
+        functools.partial(kernel, n, groups, hop, tok, cl, inner),
         out_shape=(
             jax.ShapeDtypeStruct((tok, H * DL), BF16),
             jax.ShapeDtypeStruct((tok, H * DK), BF16),
@@ -467,8 +476,8 @@
             jax.ShapeDtypeStruct((CS, DK), F32),
         ),
         in_specs=[
-            any_spec,
-            any_spec,
+            hbm_spec,
+            hbm_spec,
             vmem_spec,
             vmem_spec,
             vmem_spec,
@@ -495,9 +504,10 @@
             pltpu.VMEM((n, pr, LANES), BF16),
             pltpu.VMEM((n, pr, LANES), BF16),
             pltpu.VMEM((SLOT, WIDE), F32),
-            pltpu.VMEM((CS * SLOT, LANES), F32),
-            pltpu.VMEM((count, per, LANES), F32),
-            pltpu.VMEM((CS * SLOT, LANES), F32),
+            pltpu.VMEM((plane, own_pack, LANES), F32),
+            pltpu.VMEM((plane, own_pack, LANES), F32),
+            pltpu.VMEM((n // inner, own_pack, LANES), F32),
+            pltpu.VMEM((plane, own_pack, LANES), F32),
             pltpu.VMEM((lead, DK), BF16),
             pltpu.VMEM((reach + 1, tok, DK), BF16),
             pltpu.VMEM((reach, tok, DK), BF16),
@@ -519,9 +529,11 @@
             dma,
             dma,
             dma,
+            dma,
+            dma,
         ],
         compiler_params=pltpu.CompilerParams(
-            collective_id=0, has_side_effects=True, vmem_limit_bytes=56 * 2**20
+            collective_id=0, has_side_effects=True, vmem_limit_bytes=32 * 2**20
         ),
     )(queries[0], cotangent[0], jnp.swapaxes(latents[0], 0, 1), comp_weight, sel_idx[0], sel_count)
     return (att[None], qg[None], jnp.swapaxes(lat_grad, 0, 1)[None], weight_grad)

time: 51 us -> 51.4 us (level); the launches traced: 50.8 us -> 50.6 us
  Pallas kernels: 45.3 us -> 40.9 us
  local copies, waits for them, and re-layouts: 4.86 us -> 8.95 us
    pallas_call x1, Pallas kernels: 45.3 us -> 40.9 us  [body(): pl.pallas_call(functools.partial(kernel, n, groups, hop, tok, cl, inner),...]
    unnamed x10 -> x16, local copies, waits for them, and re-layouts: 4.86 us -> 8.95 us
where the time goes in v4:
time: 51.4 us; the launch traced here: 50.6 us
  Pallas kernels  40.9 us (80%)
  local copies, waits for them, and re-layouts  8.95 us (17%)
  between operations  0.66 us (1%)
    pallas_call x1, Pallas kernels, body(): pl.pallas_call(functools.partial(kernel, n, groups, hop, tok, cl, inner),...  40.9 us
    unnamed x16, local copies, waits for them, and re-layouts  8.95 us

profile of v4, /device:TPU:0, one launch (start us, length us, event | category | flops | bytes accessed | tf_op | source)
XLA Modules:
  0.0 50.6 jit_solution(11377266462856663492)
XLA Ops:
  0.6 0.0 copy-start
  0.6 1.3 %copy-done = bf16[1,128,4608]{2,1,0:T(8,128)(2,1)S(1)} copy-done((bf16[1,128,4608]{2,1,0:T(8,128)(2,1)S(1)}, bf16[1,128,4608]{2,1,0:T(8,128)(2,1)}, u32[]{:S(2)}) %copy-start) | copy-done | bytes 1179672
  1.9 0.0 copy-start.1
  1.9 1.2 %copy-done.1 = bf16[1,128,4096]{2,1,0:T(8,128)(2,1)S(1)} copy-done((bf16[1,128,4096]{2,1,0:T(8,128)(2,1)S(1)}, bf16[1,128,4096]{2,1,0:T(8,128)(2,1)}, u32[]{:S(2)}) %copy-start.1) | copy-done | bytes 1048600
  3.1 0.0 copy-start.2
  3.1 0.9 %copy-done.2 = bf16[1,128,576]{1,2,0:T(8,128)(2,1)S(1)} copy-done((bf16[1,128,576]{1,2,0:T(8,128)(2,1)S(1)}, bf16[1,128,576]{1,2,0:T(8,128)(2,1)}, u32[]{:S(2)}) %copy-start.2) | copy-done | bytes 147480
  4.0 0.0 copy-start.3
  4.0 0.9 %copy-done.3 = f32[32,576]{1,0:T(8,128)S(1)} copy-done((f32[32,576]{1,0:T(8,128)S(1)}, f32[32,576]{1,0:T(8,128)}, u32[]{:S(2)}) %copy-start.3) | copy-done | bytes 73752
  4.9 0.0 copy-start.4
  4.9 0.7 %copy-done.4 = s32[1,2,64]{2,1,0:T(2,128)S(1)} copy-done((s32[1,2,64]{2,1,0:T(2,128)S(1)}, s32[1,2,64]{2,1,0:T(2,128)}, u32[]{:S(2)}) %copy-start.4) | copy-done | bytes 536
  5.6 0.0 copy-start.5
  5.6 0.7 %copy-done.5 = s32[1,2]{1,0:T(1,128)S(1)} copy-done((s32[1,2]{1,0:T(1,128)S(1)}, s32[1,2]{1,0:T(1,128)}, u32[]{:S(2)}) %copy-start.5) | copy-done | bytes 32
  6.3 40.9 %shard_map.93 = (bf16[128,4096]{1,0:T(8,128)(2,1)S(1)}, bf16[128,4608]{1,0:T(8,128)(2,1)S(1)}, f32[576,128]{1,0:T(8,128)S(1)}, f32[32,576]{1,0:T(8,128)S(1)}) custom-call(bf16[128,4608]{1,0:T(8,128)(2,1)S(1)} %bitcast.11, bf16[128,4096]{1,0:T(8,128)(2,1)S(1)} %bitcast.13, bf16[576,128]{1,0:T(8,128)(2,1)S(1)} %bitcast.16, f32[32,576]{1,0:T(8,128)S(1)} %copy-done.3, ...), custom_call_target="tpu_custom_call" | custom-call | tf_op jit(solution)/shard_map/pallas_call | solution.py:470
  47.2 1.0 %copy.14 = bf16[1,128,4096]{2,1,0:T(8,128)(2,1)} copy(bf16[1,128,4096]{2,1,0:T(8,128)(2,1)S(1)} %bitcast.14) | data formatting | bytes 2097152
  48.2 1.0 %copy.15 = bf16[1,128,4608]{2,1,0:T(8,128)(2,1)} copy(bf16[1,128,4608]{2,1,0:T(8,128)(2,1)S(1)} %bitcast.12) | data formatting | bytes 2359296
  49.2 0.7 %copy.16 = f32[1,128,576]{1,2,0:T(8,128)} copy(f32[1,128,576]{1,2,0:T(8,128)S(1)} %bitcast.15) | data formatting | bytes 589824
  49.9 0.6 %copy.17 = f32[32,576]{1,0:T(8,128)} copy(f32[32,576]{1,0:T(8,128)S(1)} %get-tuple-element.19) | data formatting | bytes 147456
Async XLA Ops:
  0.6 1.3 %copy-start = (bf16[1,128,4608]{2,1,0:T(8,128)(2,1)S(1)}, bf16[1,128,4608]{2,1,0:T(8,128)(2,1)}, u32[]{:S(2)}) copy-start(bf16[1,128,4608]{2,1,0:T(8,128)(2,1)} %param.6) | copy-start | bytes 3538948
  1.9 1.2 %copy-start.1 = (bf16[1,128,4096]{2,1,0:T(8,128)(2,1)S(1)}, bf16[1,128,4096]{2,1,0:T(8,128)(2,1)}, u32[]{:S(2)}) copy-start(bf16[1,128,4096]{2,1,0:T(8,128)(2,1)} %param.8) | copy-start | bytes 3145732
  3.1 0.9 %copy-start.2 = (bf16[1,128,576]{1,2,0:T(8,128)(2,1)S(1)}, bf16[1,128,576]{1,2,0:T(8,128)(2,1)}, u32[]{:S(2)}) copy-start(bf16[1,128,576]{1,2,0:T(8,128)(2,1)} %param.7) | copy-start | bytes 442372
  4.0 0.9 %copy-start.3 = (f32[32,576]{1,0:T(8,128)S(1)}, f32[32,576]{1,0:T(8,128)}, u32[]{:S(2)}) copy-start(f32[32,576]{1,0:T(8,128)} %cw_ref.1) | copy-start | bytes 221188
  4.9 0.7 %copy-start.4 = (s32[1,2,64]{2,1,0:T(2,128)S(1)}, s32[1,2,64]{2,1,0:T(2,128)}, u32[]{:S(2)}) copy-start(s32[1,2,64]{2,1,0:T(2,128)} %param.10) | copy-start | bytes 1540
  5.6 0.7 %copy-start.5 = (s32[1,2]{1,0:T(1,128)S(1)}, s32[1,2]{1,0:T(1,128)}, u32[]{:S(2)}) copy-start(s32[1,2]{1,0:T(1,128)} %cnt_ref.1) | copy-start | bytes 28

commit v5 on v4

--- a/solution.py
+++ b/solution.py
@@ -535,7 +535,19 @@
         compiler_params=pltpu.CompilerParams(
             collective_id=0, has_side_effects=True, vmem_limit_bytes=32 * 2**20
         ),
-    )(queries[0], cotangent[0], jnp.swapaxes(latents[0], 0, 1), comp_weight, sel_idx[0], sel_count)
+    )(
+        *(
+            pltpu.with_memory_space_constraint(operand, pltpu.HBM)
+            for operand in (
+                queries[0],
+                cotangent[0],
+                jnp.swapaxes(latents[0], 0, 1),
+                comp_weight,
+                sel_idx[0],
+                sel_count,
+            )
+        )
+    )
     return (att[None], qg[None], jnp.swapaxes(lat_grad, 0, 1)[None], weight_grad)
 
 

time: 51.4 us -> 46.1 us (0.90)
  local copies, waits for them, and re-layouts: 8.95 us -> 3.33 us
    unnamed x16 -> x4, local copies, waits for them, and re-layouts: 8.95 us -> 3.33 us
where the time goes in v5:
time: 46.1 us; the launch traced here: 45.4 us
  Pallas kernels  41.4 us (90%)
  local copies, waits for them, and re-layouts  3.33 us (7%)
  between operations  0.64 us (1%)
    pallas_call x1, Pallas kernels, body(): pl.pallas_call(functools.partial(kernel, n, groups, hop, tok, cl, inner),...  41.4 us
    unnamed x4, local copies, waits for them, and re-layouts  3.33 us

profile of v5, /device:TPU:0, one launch (start us, length us, event | category | flops | bytes accessed | tf_op | source)
XLA Modules:
  0.0 45.4 jit_solution(620161226004403460)
XLA Ops:
  0.6 41.4 %shard_map.93 = (bf16[128,4096]{1,0:T(8,128)(2,1)S(1)}, bf16[128,4608]{1,0:T(8,128)(2,1)S(1)}, f32[576,128]{1,0:T(8,128)S(1)}, f32[32,576]{1,0:T(8,128)S(1)}) custom-call(bf16[128,4608]{1,0:T(8,128)(2,1)} %bitcast.14, bf16[128,4096]{1,0:T(8,128)(2,1)} %bitcast.15, bf16[576,128]{1,0:T(8,128)(2,1)} %bitcast.16, f32[32,576]{1,0:T(8,128)} %cw_ref.1, ...), custom_call_target="tpu_custom_call" | custom-call | tf_op jit(solution)/shard_map/pallas_call | solution.py:470
  42.0 1.0 %copy.14 = bf16[1,128,4096]{2,1,0:T(8,128)(2,1)} copy(bf16[1,128,4096]{2,1,0:T(8,128)(2,1)S(1)} %bitcast.12) | data formatting | bytes 2097152
  43.0 1.0 %copy.15 = bf16[1,128,4608]{2,1,0:T(8,128)(2,1)} copy(bf16[1,128,4608]{2,1,0:T(8,128)(2,1)S(1)} %bitcast.11) | data formatting | bytes 2359296
  44.0 0.7 %copy.16 = f32[1,128,576]{1,2,0:T(8,128)} copy(f32[1,128,576]{1,2,0:T(8,128)S(1)} %bitcast.13) | data formatting | bytes 589824
  44.7 0.6 %copy.17 = f32[32,576]{1,0:T(8,128)} copy(f32[32,576]{1,0:T(8,128)S(1)} %get-tuple-element.19) | data formatting | bytes 147456

commit v6 on v5

--- a/solution.py
+++ b/solution.py
@@ -277,8 +277,8 @@
     save_att = pltpu.make_async_copy(att_buf, att_ref, save_sem.at[0])
     save_att.start()
 
-    def key_pass(start):
-        size = min(256, nk - start)
+    def key_pass(start, stop):
+        size = min(256, stop - start)
         cols = pl.ds(start, size)
         even = dot_tn(ds_ref[pl.ds(0, half), cols], qq[pl.ds(0, half), :])
         odd = dot_tn(ds_ref[pl.ds(half, half), cols], qq[pl.ds(half, half), :])
@@ -315,8 +315,8 @@
 
     done = 0
     while done < cp:
-        key_pass(done)
-        done += 256
+        key_pass(done, cp)
+        done = min(done + 256, cp)
 
     def pack_one(o, c):
         for j in range(PIECES):
@@ -361,8 +361,8 @@
             ready -= 1
         if done >= nk:
             break
-        key_pass(done)
-        done += 256
+        key_pass(done, nk)
+        done = min(done + 256, nk)
 
     wait_all(crecv_buf.at[pl.ds(0, n - 1)], rc_recv)
     total = jnp.sum(crecv_buf[...].astype(F32), axis=0)
@@ -380,10 +380,6 @@
     each(plane, rank, lambda peer: part_copy(peer).start())
     precv[rank] = part[rank]
 
-    wait_all(precv.at[pl.ds(0, plane - 1)], p_recv)
-    lines[depth] = jnp.sum(precv[...], axis=0)
-    each(outer, depth, lambda peer: line_copy(peer).start())
-
     def merge(k):
         to_sibling(k, 1).wait_recv()
         wing[segment(2 * k), :] = (seg_grad(2 * k) + srecv[k].astype(F32)).astype(BF16)
@@ -394,6 +390,10 @@
             pl.when(base >= 2 * k)(lambda k=k: merge(k))
         else:
             pl.when((parity == 1) & (base >= 2 * k))(lambda k=k: merge(k))
+
+    wait_all(precv.at[pl.ds(0, plane - 1)], p_recv)
+    lines[depth] = jnp.sum(precv[...], axis=0)
+    each(outer, depth, lambda peer: line_copy(peer).start())
 
     wait_all(lines.at[pl.ds(0, outer - 1)], l_recv)
     pout[rank] = jnp.sum(lines[...], axis=0)

time: 46.1 us -> 45.8 us (level); the launches traced: 45.4 us -> 45.7 us
  no operation moved by 1% of the time
where the time goes in v6:
time: 45.8 us; the launch traced here: 45.7 us
  Pallas kernels  41.7 us (91%)
  local copies, waits for them, and re-layouts  3.33 us (7%)
  between operations  0.64 us (1%)
    pallas_call x1, Pallas kernels, body(): pl.pallas_call(functools.partial(kernel, n, groups, hop, tok, cl, inner),...  41.7 us
    unnamed x4, local copies, waits for them, and re-layouts  3.33 us

profile of v6, /device:TPU:0, one launch (start us, length us, event | category | flops | bytes accessed | tf_op | source)
XLA Modules:
  0.0 45.7 jit_solution(6773344289786632486)
XLA Ops:
  0.6 41.7 %shard_map.93 = (bf16[128,4096]{1,0:T(8,128)(2,1)S(1)}, bf16[128,4608]{1,0:T(8,128)(2,1)S(1)}, f32[576,128]{1,0:T(8,128)S(1)}, f32[32,576]{1,0:T(8,128)S(1)}) custom-call(bf16[128,4608]{1,0:T(8,128)(2,1)} %bitcast.14, bf16[128,4096]{1,0:T(8,128)(2,1)} %bitcast.15, bf16[576,128]{1,0:T(8,128)(2,1)} %bitcast.16, f32[32,576]{1,0:T(8,128)} %cw_ref.1, ...), custom_call_target="tpu_custom_call" | custom-call | tf_op jit(solution)/shard_map/pallas_call | solution.py:470
  42.3 1.0 %copy.14 = bf16[1,128,4096]{2,1,0:T(8,128)(2,1)} copy(bf16[1,128,4096]{2,1,0:T(8,128)(2,1)S(1)} %bitcast.12) | data formatting | bytes 2097152
  43.3 1.0 %copy.15 = bf16[1,128,4608]{2,1,0:T(8,128)(2,1)} copy(bf16[1,128,4608]{2,1,0:T(8,128)(2,1)S(1)} %bitcast.11) | data formatting | bytes 2359296
  44.3 0.7 %copy.16 = f32[1,128,576]{1,2,0:T(8,128)} copy(f32[1,128,576]{1,2,0:T(8,128)S(1)} %bitcast.13) | data formatting | bytes 589824
  45.0 0.6 %copy.17 = f32[32,576]{1,0:T(8,128)} copy(f32[32,576]{1,0:T(8,128)S(1)} %get-tuple-element.19) | data formatting | bytes 147456
